TPU v7x, 256 devices: a whole 4x4x8 slice. The times are simulated.
256 devices in a mesh: lat: 8 (over x, core), lon: 16 (over z, y_lo), dp: 2 (over y_hi).
Axes of the slice: x: 4, y: 4 (y_hi: 2, y_lo: 2; y = y_hi * 2 + y_lo), z: 8, core: 2. Of those that a mesh axis runs over, the one named last changes fastest.
Arguments:
- node_latent: bfloat16 [2, 8, 16, 256, 512], P('dp', 'lat', 'lon'), may hold values from -6 to 6
- edge_latent: bfloat16 [2, 8, 16, 384, 512], P('dp', 'lat', 'lon'), may hold values from -6 to 6
- senders: int32 [8, 16, 384], P('lat', 'lon'), may hold values from 0 to 1791, as said below
- receivers: int32 [8, 16, 384], P('lat', 'lon'), may hold values from 0 to 255
- edge_live: int32 [8, 16, 384], P('lat', 'lon'), may hold values 0 or 1
- halo_list: int32 [8, 16, 128], P('lat', 'lon'), may hold values from 0 to 255
- coarse_list: int32 [8, 16, 8], P('lat', 'lon'), may hold values from 0 to 255
- edge_in_w: bfloat16 [1536, 512], replicated, may hold values from -0.15625 to 0.15625
- edge_out_w: bfloat16 [512, 512], replicated, may hold values from -0.25 to 0.25
- node_in_w: bfloat16 [1024, 512], replicated, may hold values from -0.1875 to 0.1875
- node_out_w: bfloat16 [512, 512], replicated, may hold values from -0.25 to 0.25
- edge_gain: float32 [512], replicated, may hold values from 0.25 to 1.75
- node_gain: float32 [512], replicated, may hold values from 0.25 to 1.75
- node_cot: bfloat16 [2, 8, 16, 256, 512], P('dp', 'lat', 'lon'), may hold values from -6 to 6
- edge_cot: bfloat16 [2, 8, 16, 384, 512], P('dp', 'lat', 'lon'), may hold values from -6 to 6
Outputs:
- new_nodes: bfloat16 [2, 8, 16, 256, 512], P('dp', 'lat', 'lon')
- new_edges: bfloat16 [2, 8, 16, 384, 512], P('dp', 'lat', 'lon')
- node_grad: bfloat16 [2, 8, 16, 256, 512], P('dp', 'lat', 'lon')
- edge_grad: bfloat16 [2, 8, 16, 384, 512], P('dp', 'lat', 'lon')
- weight_grad: float32 [1835008], P(('lat', 'lon', 'dp'))
- gain_grad: float32 [2, 512], replicated
Inputs may be any that keep to these rules, and one draw needn't show every extreme that they name: `senders`: rows below 256 are own nodes, the next 512 rows the lower, upper, west and east rim lists, the rest the coarse rows.
All inputs are finite; a program needn't handle non-finite values. No bound on the sum of `edge_live` on one device may be relied on, other than what follows from the above.
Results may differ from a plain program's by a relative error of at most 0.015.
Values may be sent and summed in bfloat16 or wider, within the bound.
No kernel may reach another device: no remote copies, remote signals or barrier semaphores. Data moves between devices by JAX's collectives and lax.ppermute only.
A program may use at most 128 MiB of HBM per device.

v0:
```python
import functools

import jax
import jax.numpy as jnp
from jax import lax
from jax.sharding import PartitionSpec as P


def shifted(block, axis, distance):
    devices = range(lax.axis_size(axis))
    route = [(i - distance, i) for i in devices if i - distance in devices]
    return lax.ppermute(block, axis, route)


def from_behind(value, axis, steps):
    count = lax.axis_size(axis)
    pairs = [(source, (source + steps) % count) for source in range(count)]
    return lax.ppermute(value, axis, pairs)


def layer_norm(values, gain):
    center = values - jnp.mean(values, axis=-1, keepdims=True)
    spread = jnp.mean(center * center, axis=-1, keepdims=True)
    return center * lax.rsqrt(spread + 1e-05) * gain


def local_layer(send, recv, live, table, own, edges, w_ein, w_eout, w_nin, w_nout, gain_e, gain_n):
    count = own.shape[0]
    from_send = jnp.take(table, send, axis=0)
    from_recv = jnp.take(own, recv, axis=0)
    joined = jnp.concatenate([from_send, from_recv, edges], axis=-1).astype(jnp.bfloat16)
    hidden = jax.nn.silu(jnp.dot(joined, w_ein, preferred_element_type=jnp.float32)).astype(
        jnp.bfloat16
    )
    message = layer_norm(jnp.dot(hidden, w_eout, preferred_element_type=jnp.float32), gain_e)
    new_edge = (edges + message).astype(jnp.bfloat16)
    pooled = jax.ops.segment_sum(
        message * live[:, None].astype(jnp.float32), recv, num_segments=count
    )
    node_input = jnp.concatenate([own, pooled], axis=-1).astype(jnp.bfloat16)
    node_hidden = jax.nn.silu(
        jnp.dot(node_input, w_nin, preferred_element_type=jnp.float32)
    ).astype(jnp.bfloat16)
    update = layer_norm(jnp.dot(node_hidden, w_nout, preferred_element_type=jnp.float32), gain_n)
    new_node = (own + update).astype(jnp.bfloat16)
    return (new_node, new_edge)


def on_device(
    node_latent,
    edge_latent,
    senders,
    receivers,
    edge_live,
    halo_list,
    coarse_list,
    edge_in_w,
    edge_out_w,
    node_in_w,
    node_out_w,
    edge_gain,
    node_gain,
    node_cot,
    edge_cot,
):
    nodes_bf = node_latent[0, 0, 0]
    own = nodes_bf.astype(jnp.float32)
    edges32 = edge_latent[0, 0, 0].astype(jnp.float32)
    send = senders[0, 0]
    recv = receivers[0, 0]
    live = edge_live[0, 0]
    rim_list = halo_list[0, 0]
    coarse_ids = coarse_list[0, 0]
    count = own.shape[0]
    rim_rows = rim_list.shape[0]
    outgoing = jnp.take(nodes_bf, rim_list, axis=0)
    received = []
    for step_by in (1, -1):
        received.append(shifted(outgoing, "lat", step_by))
    for step_by in (1, -1):
        received.append(from_behind(outgoing, "lon", step_by))
    coarse_own = jnp.take(nodes_bf, coarse_ids, axis=0)
    coarse_all = lax.all_gather(coarse_own, ("lat", "lon"), axis=0, tiled=True)
    table = jnp.concatenate(
        [own]
        + [piece.astype(jnp.float32) for piece in received]
        + [coarse_all.astype(jnp.float32)],
        axis=0,
    )
    layer = functools.partial(local_layer, send, recv, live)
    primal, pullback = jax.vjp(
        layer,
        table,
        own,
        edges32,
        edge_in_w,
        edge_out_w,
        node_in_w,
        node_out_w,
        edge_gain,
        node_gain,
    )
    grads = pullback((node_cot[0, 0, 0], edge_cot[0, 0, 0]))
    table_grad = grads[0]
    own_grad = grads[1] + table_grad[:count]
    rim_grads = [table_grad[count + k * rim_rows : count + (k + 1) * rim_rows] for k in range(4)]
    returned = jnp.zeros((rim_rows, own.shape[1]), jnp.float32)
    for step_by, piece in ((1, rim_grads[0]), (-1, rim_grads[1])):
        returned = returned + shifted(piece.astype(jnp.bfloat16), "lat", -step_by).astype(
            piece.dtype
        )
    for step_by, piece in ((1, rim_grads[2]), (-1, rim_grads[3])):
        returned = returned + from_behind(piece.astype(jnp.bfloat16), "lon", -step_by).astype(
            piece.dtype
        )
    own_grad = own_grad + jax.ops.segment_sum(returned, rim_list, num_segments=count)
    coarse_grad_all = table_grad[count + 4 * rim_rows :]
    coarse_mine = lax.psum_scatter(coarse_grad_all, ("lat", "lon"), scatter_dimension=0, tiled=True)
    own_grad = own_grad + jax.ops.segment_sum(coarse_mine, coarse_ids, num_segments=count)
    devices = lax.axis_size("lat") * lax.axis_size("lon") * lax.axis_size("dp")
    factor = 1.0 / jnp.sqrt(jnp.float32(send.shape[0] * devices))
    flat = jnp.concatenate(
        [
            grads[3].astype(jnp.float32).reshape(-1),
            grads[4].astype(jnp.float32).reshape(-1),
            grads[5].astype(jnp.float32).reshape(-1),
            grads[6].astype(jnp.float32).reshape(-1),
        ]
    )
    weight_share = lax.psum_scatter(flat, ("lat", "lon", "dp"), scatter_dimension=0, tiled=True)
    edge_gain_sum, node_gain_sum = lax.psum((grads[7], grads[8]), ("lat", "lon", "dp"))
    gain_grad = jnp.stack([edge_gain_sum, node_gain_sum]) * factor
    new_nodes = primal[0][None, None, None]
    new_edges = primal[1][None, None, None]
    node_grad = own_grad.astype(jnp.bfloat16)[None, None, None]
    edge_grad = grads[2].astype(jnp.bfloat16)[None, None, None]
    return (new_nodes, new_edges, node_grad, edge_grad, weight_share * factor, gain_grad)


def solution(mesh):
    placed = (
        P("dp", "lat", "lon", None, None),
        P("dp", "lat", "lon", None, None),
        P("lat", "lon", None),
        P("lat", "lon", None),
        P("lat", "lon", None),
        P("lat", "lon", None),
        P("lat", "lon", None),
        P(),
        P(),
        P(),
        P(),
        P(),
        P(),
        P("dp", "lat", "lon", None, None),
        P("dp", "lat", "lon", None, None),
    )
    return jax.shard_map(
        on_device,
        mesh=mesh,
        in_specs=placed,
        out_specs=(
            P("dp", "lat", "lon", None, None),
            P("dp", "lat", "lon", None, None),
            P("dp", "lat", "lon", None, None),
            P("dp", "lat", "lon", None, None),
            P(("lat", "lon", "dp")),
            P(),
        ),
        check_vma=False,
    )
```

profile of v0, /device:TPU:16, one launch (start us, length us, event | category | flops | bytes accessed | tf_op | source)
XLA Modules:
  0.0 1288.2 jit_solution(8439464802548380759)
XLA Ops:
  7.2 0.8 fusion.59
  9.4 1.9 gather_fusion
  11.3 1.7 collective-permute-start
  13.1 1.3 collective-permute-start.1
  14.4 1.4 collective-permute-start.2
  15.7 5.4 collective-permute-start.3
  21.1 0.7 compare_and_fusion.2
  21.8 1.6 gather_fusion.1
  23.3 0.7 broadcast_select_fusion.1
  24.1 0.7 fusion.57
  24.8 0.7 reduce
  25.5 0.7 fusion.56
  26.2 0.7 reduce.1
  26.9 2.1 gather_fusion.3
  29.0 0.7 convert_dynamic-update-slice_fusion.5
  29.9 0.7 convert_dynamic-update-slice_fusion.4
  32.6 344.6 %all-gather.2.cloned.1.call-done = bf16[1024,512]{1,0:T(8,128)(2,1)} async-done(((bf16[8,512]{1,0:T(8,128)(2,1)}), bf16[1024,512]{1,0:T(8,128)(2,1)}) %all-gather.2.cloned.1.call-update) | async-done | bytes 1048592 | tf_op jit(solution)/shard_map/all_gather | solution.py:83
  377.2 2.3 convert_dynamic-update-slice_fusion
  379.5 3.9 gather_fusion.2
  383.6 0.8 fusion.32
  386.0 3.6 scatter_custom_fusion
  389.7 1.7 fusion.41
  392.7 1.0 fusion.68
  394.1 1.2 fusion.8
  395.8 1.5 fusion.4
  397.3 2.2 gather_fusion.4
  399.5 1.7 multiply_reduce_fusion
  401.3 1.3 fusion.67
  405.7 1.0 fusion.3
  406.7 0.8 copy.21
  407.5 26.3 %maximum_convert_fusion = f32[1835008]{0:T(1024)} fusion(bf16[262144]{0:T(1024)(128)(2,1)S(1)} %bitcast.82, bf16[524288]{0:T(1024)(128)(2,1)S(1)} %bitcast.81, bf16[262144]{0:T(1024)(128)(2,1)S(1)} %bitcast.83, bf16[786432]{0:T(1024)(128)(2,1)S(1)} %bitcast.80), kind=kLoop, calls=%fused_computation.10 | loop fusion | flops 14680064 | bytes 11010048 | tf_op jit(solution)/shard_map/concatenate | solution.py:122
  433.9 2.2 fusion
  436.1 5.4 scatter_custom_fusion.1
  441.5 3.1 slice.43
  444.7 2.4 convert.28
  447.2 4.1 collective-permute-start.6
  451.3 1.3 collective-permute-start.5
  452.6 1.3 collective-permute-start.4
  454.0 1.2 fusion.28
  455.1 2.0 fusion.34
  457.1 3.7 scatter_custom_fusion.2
  460.8 79.1 %all-reduce.1 = (f32[1,512]{1,0:T(1,128)S(1)}, f32[1,512]{1,0:T(1,128)S(1)}) all-reduce(f32[1,512]{1,0:T(1,128)S(1)} %bitcast.86, f32[1,512]{1,0:T(1,128)S(1)} %bitcast.87), channel_id=1, replica_groups=mesh['lat'=8,'lon'=16,'dp'=2] {'lat','lon','dp'}, use_global_device_ids=true, to_apply=%region_18.19 | all-reduce | flops 1024 | bytes 8192 | tf_op jit(solution)/shard_map/psum | solution.py:131
  541.9 2.0 scatter_custom_fusion.3
  543.9 168.6 %all-reduce.4.cloned.1.call-done = f32[1835008]{0:T(1024)} async-done(((f32[1835008]{0:T(1024)}), f32[1835008]{0:T(1024)}) %all-reduce.4.cloned.1.call-update) | async-done | bytes 7340048
  712.5 1.4 dynamic-slice_multiply_fusion
  713.9 565.8 %reduce-scatter.2.cloned.1.call-done = f32[8,512]{1,0:T(8,128)} async-done(((f32[1024,512]{1,0:T(8,128)}), f32[8,512]{1,0:T(8,128)}) %reduce-scatter.2.cloned.1.call-update) | async-done | bytes 16400 | tf_op jit(solution)/shard_map/reduce_scatter | solution.py:118
  1279.6 1.0 scatter_fusion
  1280.7 0.7 convert_bitcast_fusion
  (110 shorter events, 12.9 us)
Async XLA Ops:
  7.2 376.4 %copy-start = (bf16[1536,512]{1,0:T(8,128)(2,1)S(1)}, bf16[1536,512]{1,0:T(8,128)(2,1)}, u32[]{:S(2)}) copy-start(bf16[1536,512]{1,0:T(8,128)(2,1)} %param.22) | copy-start | bytes 4718596
  7.2 19.7 %copy-start.1 = (bf16[1,1,1,256,512]{4,3,2,1,0:T(8,128)(2,1)S(1)}, bf16[1,1,1,256,512]{4,3,2,1,0:T(8,128)(2,1)}, u32[]{:S(2)}) copy-start(bf16[1,1,1,256,512]{4,3,2,1,0:T(8,128)(2,1)} %param.15) | copy-start | bytes 786436
  7.2 370.1 %all-gather.2.cloned.1.call-start = ((), (), s32[]{:S(2)}) async-start(), calls=%async_computation.1 | async-start | bytes 1056768 | tf_op jit(solution)/shard_map/all_gather | solution.py:83
  11.3 18.6 %collective-permute-start = (bf16[128,512]{1,0:T(8,128)(2,1)S(1)}, bf16[128,512]{1,0:T(8,128)(2,1)S(1)}, u32[]{:S(2)}, u32[]{:S(2)}) collective-permute-start(bf16[128,512]{1,0:T(8,128)(2,1)S(1)} %broadcast_select_fusion), channel_id=1, source_target_pairs={{0,32},{32,64},{64,96},{96,128},{128,160},{160,192},{192,224},{1,3... | collective-permute-start | bytes 393224 | tf_op jit(solution)/shard_map/ppermute | solution.py:12
  13.1 17.6 %collective-permute-start.1 = (bf16[128,512]{1,0:T(8,128)(2,1)S(1)}, bf16[128,512]{1,0:T(8,128)(2,1)S(1)}, u32[]{:S(2)}, u32[]{:S(2)}) collective-permute-start(bf16[128,512]{1,0:T(8,128)(2,1)S(1)} %broadcast_select_fusion), channel_id=1, source_target_pairs={{32,0},{64,32},{96,64},{128,96},{160,128},{192,160},{224,192},{33,... | collective-permute-start | bytes 393224 | tf_op jit(solution)/shard_map/ppermute | solution.py:12
  14.4 17.0 %collective-permute-start.2 = (bf16[128,512]{1,0:T(8,128)(2,1)S(1)}, bf16[128,512]{1,0:T(8,128)(2,1)S(1)}, u32[]{:S(2)}, u32[]{:S(2)}) collective-permute-start(bf16[128,512]{1,0:T(8,128)(2,1)S(1)} %broadcast_select_fusion), channel_id=1, source_target_pairs={{0,2},{2,4},{4,6},{6,8},{8,10},{10,12},{12,14},{14,16},{16,18},{18... | collective-permute-start | bytes 393224 | tf_op jit(solution)/shard_map/ppermute | solution.py:18
  15.7 16.3 %collective-permute-start.3 = (bf16[128,512]{1,0:T(8,128)(2,1)S(1)}, bf16[128,512]{1,0:T(8,128)(2,1)S(1)}, u32[]{:S(2)}, u32[]{:S(2)}) collective-permute-start(bf16[128,512]{1,0:T(8,128)(2,1)S(1)} %broadcast_select_fusion), channel_id=1, source_target_pairs={{0,30},{2,0},{4,2},{6,4},{8,6},{10,8},{12,10},{14,12},{16,14},{18,... | collective-permute-start | bytes 393224 | tf_op jit(solution)/shard_map/ppermute | solution.py:18
  24.0 688.5 %all-reduce.4.cloned.1.call-start = ((), (), s32[]{:S(2)}) async-start(), calls=%async_computation.3 | async-start | bytes 14680064
  26.9 3.0 copy-start.21
  29.9 353.7 %copy-start.13 = (bf16[384,512]{1,0:T(8,128)(2,1)}, bf16[384,512]{1,0:T(8,128)(2,1)S(1)}, u32[]{:S(2)}) copy-start(bf16[384,512]{1,0:T(8,128)(2,1)S(1)} %select_convert_fusion) | copy-start | bytes 1179652
  379.5 4.1 copy-start.11
  383.6 0.8 copy-start.15
  383.6 1.2 copy-start.24
  384.8 0.9 copy-start.26
  384.8 1.2 copy-start.19
  389.6 1.8 copy-start.23
  391.4 1.0 copy-start.7
  391.4 0.9 copy-start.20
  394.1 1.2 copy-start.9
  395.8 1.5 copy-start.3
  397.3 2.3 copy-start.6
  399.5 1.7 copy-start.2
  399.5 1.7 copy-start.12
  401.2 1.3 copy-start.25
  401.2 1.3 copy-start.27
  403.1 1.0 copy-start.10
  403.2 1.4 copy-start.5
  404.5 1.0 copy-start.14
  404.5 1.1 copy-start.16
  433.8 845.8 %reduce-scatter.2.cloned.1.call-start = ((), (), s32[]{:S(2)}) async-start(), calls=%async_computation.2 | async-start | bytes 2113536 | tf_op jit(solution)/shard_map/reduce_scatter | solution.py:118
  444.7 9.3 copy-start.4
  444.7 9.3 copy-start.8
  447.1 93.4 %collective-permute-start.7 = (bf16[128,512]{1,0:T(8,128)(2,1)S(1)}, bf16[128,512]{1,0:T(8,128)(2,1)S(1)}, u32[]{:S(2)}, u32[]{:S(2)}) collective-permute-start(bf16[128,512]{1,0:T(8,128)(2,1)S(1)} %get-tuple-element.17), channel_id=1, source_target_pairs={{0,2},{2,4},{4,6},{6,8},{8,10},{10,12},{12,14},{14,16},{16,18},{18... | collective-permute-start | bytes 393224 | tf_op jit(solution)/shard_map/ppermute | solution.py:18
  447.2 93.3 %collective-permute-start.6 = (bf16[128,512]{1,0:T(8,128)(2,1)S(1)}, bf16[128,512]{1,0:T(8,128)(2,1)S(1)}, u32[]{:S(2)}, u32[]{:S(2)}) collective-permute-start(bf16[128,512]{1,0:T(8,128)(2,1)S(1)} %get-tuple-element.18), channel_id=1, source_target_pairs={{0,30},{2,0},{4,2},{6,4},{8,6},{10,8},{12,10},{14,12},{16,14},{18,... | collective-permute-start | bytes 393224 | tf_op jit(solution)/shard_map/ppermute | solution.py:18
  451.3 89.2 %collective-permute-start.5 = (bf16[128,512]{1,0:T(8,128)(2,1)S(1)}, bf16[128,512]{1,0:T(8,128)(2,1)S(1)}, u32[]{:S(2)}, u32[]{:S(2)}) collective-permute-start(bf16[128,512]{1,0:T(8,128)(2,1)S(1)} %get-tuple-element.19), channel_id=1, source_target_pairs={{0,32},{32,64},{64,96},{96,128},{128,160},{160,192},{192,224},{1,3... | collective-permute-start | bytes 393224 | tf_op jit(solution)/shard_map/ppermute | solution.py:12
  452.6 87.9 %collective-permute-start.4 = (bf16[128,512]{1,0:T(8,128)(2,1)S(1)}, bf16[128,512]{1,0:T(8,128)(2,1)S(1)}, u32[]{:S(2)}, u32[]{:S(2)}) collective-permute-start(bf16[128,512]{1,0:T(8,128)(2,1)S(1)} %get-tuple-element.16), channel_id=1, source_target_pairs={{32,0},{64,32},{96,64},{128,96},{160,128},{192,160},{224,192},{33,... | collective-permute-start | bytes 393224 | tf_op jit(solution)/shard_map/ppermute | solution.py:12
  457.1 822.5 %copy-start.22 = (s32[1,1,8]{2,1,0:T(1,128)S(1)}, s32[1,1,8]{2,1,0:T(1,128)}, u32[]{:S(2)}) copy-start(s32[1,1,8]{2,1,0:T(1,128)} %param.21) | copy-start | bytes 100
  540.6 0.7 copy-start.17
  541.2 0.6 copy-start.18
Sparse Core Ops, SparseCore 0:
  24.2 353.0 all-gather.1
  434.0 278.5 all-reduce.3
  715.0 564.5 reduce-scatter.1
where the time goes:
time: 1300 us; the launch traced here: 1290 us
  waiting for transfers between devices  1080 us (83%)
  blocking collectives  79.1 us (6%)
  other arithmetic  67.6 us (5%)
  local copies, waits for them, and re-layouts  20 us (2%)
  starting transfers between devices  16.7 us (1%)
  between operations  14.6 us (1%)
    reduce_scatter x1, waiting for transfers between devices, on_device(): lax.psum_scatter(coarse_grad_all, ('lat', 'lon'), scatter_dimension=0, ti...  566 us
    all_gather x1, waiting for transfers between devices, on_device(): coarse_all = lax.all_gather(coarse_own, ('lat', 'lon'), axis=0, tiled=True)  345 us
    unnamed x4, waiting for transfers between devices  169 us
    psum x1, blocking collectives, on_device(): lax.psum((grads[7], grads[8]), ('lat', 'lon', 'dp'))  79.1 us
    concatenate x1, other arithmetic, on_device(): jnp.concatenate([grads[3].astype(jnp.float32).reshape(-1), grads[4].astyp...  26.3 us
  transfers between devices with their start and end apart: 11, of which 3 were waited for; matrix products, arithmetic and copies ran while one was open for 3% of the time, Pallas kernels for 0%

commit v1 on v0

v1 whole, which is shorter than its diff:
```python
import functools
import math

import jax
import jax.numpy as jnp
from jax import lax
from jax.experimental import pallas as pl
from jax.experimental.pallas import tpu as pltpu
from jax.sharding import PartitionSpec as P

AXES = ("lat", "lon", "dp")
F32 = jnp.float32
BF16 = jnp.bfloat16
WIDTH = 512
UNIT = 304


def shifted(block, axis, distance):
    devices = range(lax.axis_size(axis))
    route = [(i - distance, i) for i in devices if i - distance in devices]
    return lax.ppermute(block, axis, route)


def from_behind(value, axis, steps):
    count = lax.axis_size(axis)
    pairs = [(source, (source + steps) % count) for source in range(count)]
    return lax.ppermute(value, axis, pairs)


def partner_of(index, kind, amount):
    x, core, z = index >> 6, index >> 5 & 1, index >> 2 & 7
    y_lo, y_hi = index >> 1 & 1, index & 1
    if kind == "core":
        core ^= 1
    elif kind == "x":
        x ^= amount
    elif kind == "z":
        z ^= amount
    elif kind == "ring":
        z = (z - amount if z & 1 else z + amount) & 7
    elif kind == "y":
        y_lo ^= amount & 1
        y_hi ^= amount >> 1
    return ((x * 2 + core) * 8 + z) * 4 + y_lo * 2 + y_hi


def exchange(value, kind, amount=1):
    pairs = [(i, partner_of(i, kind, amount)) for i in range(256)]
    return lax.ppermute(value, AXES, pairs)


def position():
    lat, lon, dp = (lax.axis_index(axis) for axis in AXES)
    return lat >> 1, lat & 1, lon >> 1, lon & 1, dp


def doubled(rows, *stages):
    for kind, amount in stages:
        rows = jnp.concatenate([rows, exchange(rows, kind, amount)], axis=0)
    return rows


def coarse_slot(row):
    x, core, z, y_lo, _ = position()
    owner, within = row >> 3, row & 7
    dx = (owner >> 5) ^ x
    dcore = (owner >> 4 & 1) ^ core
    ahead = ((owner >> 1 & 7) - z) * (1 - 2 * (z & 1)) & 7
    zslot = 0x23764510 >> (4 * ahead) & 7
    dy = (owner & 1) ^ y_lo
    high, mixed = dx >> 1, (dx ^ dx >> 1) & 1
    half = zslot >> 2
    xslot = jnp.where(half == 0, high * 2 + mixed, mixed * 2 + high)
    return dcore * 512 + half * 256 + xslot * 64 + (zslot & 3) * 16 + dy * 8 + within


def plus(*values):
    total = values[0].astype(F32)
    for value in values[1:]:
        total = lax.reduce_precision(total + value.astype(F32), 8, 7)
    return total.astype(BF16)


def pick(array, which, axis=0):
    return lax.dynamic_index_in_dim(array, which, axis, keepdims=False)


def reduce_all(keep_far, send_far, keep_near, send_near, rim_grad):
    _, _, z, y_lo, y_hi = position()
    got_far = exchange(send_far, "core")
    got_near = exchange(send_near, "core")
    got_a = exchange(plus(keep_far[0], got_far[0]), "x", 3)
    got_b = exchange(plus(keep_far[1], got_far[1]), "x", 1)
    back_lon = [from_behind(rim_grad[128 * k : 128 * k + 128], "lon", step) for k, step in ((2, -1), (3, 1))]
    got_a, got_b, *back_lon = lax.optimization_barrier((got_a, got_b, *back_lon))
    new_a = exchange(plus(keep_near[0, 1], got_near[0, 1], got_a[1]), "x", 1)
    new_b = exchange(plus(keep_near[1, 1], got_near[1, 1], got_b[1]), "x", 3)
    new_a, new_b, rim_grad = lax.optimization_barrier((new_a, new_b, rim_grad))
    back_lat = [shifted(rim_grad[128 * k : 128 * k + 128], "lat", step) for k, step in ((0, -1), (1, 1))]
    a = plus(keep_near[0, 0], got_near[0, 0], got_a[0], new_a)
    b = plus(keep_near[1, 0], got_near[1, 0], got_b[0], new_b)
    weights = jnp.concatenate([a[:224], b[:224]], axis=0).reshape(8, 4, 14, WIDTH)
    gains = jnp.broadcast_to(a[288:290], (8, 4, 2, WIDTH))
    coarse = jnp.concatenate([a[224:288], b[224:288]], axis=0).reshape(8, 2, 8, WIDTH)
    units = jnp.concatenate([weights, gains], axis=2).reshape(8, 2, 2, 16, WIDTH)
    got = exchange(pick(units, 1 - y_hi, 2), "y", 3)
    units = plus(pick(units, y_hi, 2), got)
    units = jnp.concatenate([units, coarse], axis=2)
    got = exchange(pick(units, 1 - y_lo, 1), "y", 1)
    units = plus(pick(units, y_lo, 1), got).reshape(2, 2, 2, 24, WIDTH)
    units, *back_lat = lax.optimization_barrier((units, *back_lat))
    got = exchange(pick(units, 1 - (z & 1), 2), "z", 1)
    units = plus(pick(units, z & 1, 2), got)
    got = exchange(pick(units, 1 - (z >> 1 & 1), 1), "z", 2)
    units = plus(pick(units, z >> 1 & 1, 1), got)
    got = exchange(pick(units, 1 - (z >> 2)), "z", 4)
    return pick(units, z >> 2), got, back_lat + back_lon


def dot(a, b, ca=1, cb=0):
    return lax.dot_general(a, b, (((ca,), (cb,)), ((), ())), preferred_element_type=F32)


def down(row, count):
    return jnp.broadcast_to(row, (128, count)).T


def one_hot(columns, first, width):
    lane = lax.broadcasted_iota(jnp.int32, columns.shape, 1)
    tiles = [columns == lane + (first + at) for at in range(0, width, 128)]
    return jnp.concatenate([tile.astype(F32).astype(BF16) for tile in tiles], axis=1)


def one_hot_t(row, first, height):
    at = lax.broadcasted_iota(jnp.int32, (height, row.shape[1]), 0) + first
    return (at == row).astype(F32).astype(BF16)


def normed(values):
    center = values - jnp.mean(values, axis=-1, keepdims=True)
    spread = jnp.mean(center * center, axis=-1, keepdims=True)
    scale = lax.rsqrt(spread + 1e-05)
    return center * scale, scale


def normed_back(grad, unit, scale):
    inner = jnp.mean(grad * unit, axis=-1, keepdims=True)
    return scale * (grad - jnp.mean(grad, axis=-1, keepdims=True) - unit * inner)


def silu_slope(pre):
    gate = jax.nn.sigmoid(pre)
    return gate * (1.0 + pre * (1.0 - gate))


def outgoing_kernel(rim_ref, coarse_ref, nodes_ref, rows_ref, coarse_rows_ref):
    nodes = nodes_ref[...]
    rows_ref[...] = dot(one_hot(down(rim_ref[...], 128), 0, 256), nodes).astype(BF16)
    coarse_rows_ref[...] = dot(one_hot_t(coarse_ref[...], 0, 256), nodes, 0, 0).astype(BF16)


def fetch(pairs, sems):
    copies = [pltpu.make_async_copy(src, dst, sems.at[n]) for n, (src, dst) in enumerate(pairs)]
    for copy in copies:
        copy.start()
    return lambda n: copies[n].wait()


def near_kernel(
    index_ref,
    nodes_hbm,
    edges_hbm,
    w_ein_hbm,
    w_nin_hbm,
    pre_ref,
    node_pre_ref,
    recv_rows_ref,
    own_rows_ref,
    nodes_ref,
    edges_ref,
    w_ein_ref,
    w_nin_ref,
    sems,
):
    wait = fetch(
        (
            (nodes_hbm, nodes_ref),
            (w_ein_hbm, w_ein_ref),
            (edges_hbm, edges_ref),
            (w_nin_hbm.at[0:512], w_nin_ref),
        ),
        sems,
    )
    slots = one_hot(down(index_ref[0:1], 384), 0, 256)
    receivers = one_hot(down(index_ref[2:3], 384), 0, 256)
    wait(0)
    nodes = nodes_ref[...]
    recv_rows = dot(receivers, nodes).astype(BF16)
    own_rows = dot(slots, nodes).astype(BF16)
    recv_rows_ref[...] = recv_rows
    own_rows_ref[...] = own_rows
    wait(1)
    wait(2)
    pre_ref[...] = (
        dot(own_rows, w_ein_ref[0:512])
        + dot(recv_rows, w_ein_ref[512:1024])
        + dot(edges_ref[...], w_ein_ref[1024:1536])
    )
    wait(3)
    node_pre_ref[...] = dot(nodes, w_nin_ref[...])


def layer_kernel(
    place_ref,
    index_ref,
    pre_ref,
    node_pre_ref,
    recv_rows_ref,
    own_rows_ref,
    edges_hbm,
    nodes_hbm,
    lower_ref,
    upper_ref,
    west_ref,
    east_ref,
    near_top_ref,
    near_low_ref,
    far_top_ref,
    far_low_ref,
    w_ein_hbm,
    w_eout_hbm,
    w_nin_hbm,
    w_nout_hbm,
    gain_e_ref,
    gain_n_ref,
    node_cot_hbm,
    edge_cot_hbm,
    new_nodes_hbm,
    new_edges_hbm,
    edge_grad_hbm,
    own_grad_hbm,
    rim_grad_ref,
    keep_far_ref,
    send_far_ref,
    keep_near_ref,
    send_near_ref,
    big_ref,
    coarse_ref,
    unit_ref,
    edges_ref,
    nodes_ref,
    w_ein_ref,
    w_eout_ref,
    w_nin_ref,
    w_nout_ref,
    node_cot_ref,
    edge_cot_ref,
    new_nodes_ref,
    new_edges_ref,
    edge_grad_ref,
    own_grad_ref,
    sems,
    out_sems,
):
    wait = fetch(
        (
            (w_ein_hbm, w_ein_ref),
            (w_eout_hbm, w_eout_ref),
            (edges_hbm, edges_ref),
            (w_nin_hbm, w_nin_ref),
            (w_nout_hbm, w_nout_ref),
            (nodes_hbm, nodes_ref),
            (node_cot_hbm, node_cot_ref),
            (edge_cot_hbm, edge_cot_ref),
        ),
        sems,
    )
    slots = down(index_ref[0:1], 384)
    lower_upper = jnp.concatenate([lower_ref[...], upper_ref[...]], axis=0)
    west_east = jnp.concatenate([west_ref[...], east_ref[...]], axis=0)
    far = (
        dot(one_hot(slots, 256, 256), lower_upper)
        + dot(one_hot(slots, 512, 256), west_east)
        + dot(one_hot(slots, 768, 256), near_top_ref[...])
        + dot(one_hot(slots, 1024, 256), near_low_ref[...])
        + dot(one_hot(slots, 1280, 256), far_top_ref[...])
        + dot(one_hot(slots, 1536, 256), far_low_ref[...])
    ).astype(BF16)
    send_rows = (far.astype(F32) + own_rows_ref[...].astype(F32)).astype(BF16)
    wait(0)
    pre = pre_ref[...] + dot(far, w_ein_ref[0:512])
    hidden = (pre * jax.nn.sigmoid(pre)).astype(BF16)
    gain_e = gain_e_ref[...]
    wait(1)
    unit, scale = normed(dot(hidden, w_eout_ref[...]))
    unit_ref[...] = unit
    message = unit * gain_e
    wait(2)
    new_edges_ref[...] = (edges_ref[...].astype(F32) + message).astype(BF16)
    new_edges_out = pltpu.make_async_copy(new_edges_ref, new_edges_hbm, out_sems.at[0])
    new_edges_out.start()
    into = one_hot_t(index_ref[3:4], 0, 256)
    coarse_part = message.astype(BF16)
    fine_part = (message - coarse_part.astype(F32)).astype(BF16)
    pooled = (dot(into, coarse_part) + dot(into, fine_part)).astype(BF16)
    for n in (3, 4, 5, 6, 7):
        wait(n)
    nodes = nodes_ref[...]
    gain_n = gain_n_ref[...]
    node_pre = node_pre_ref[...] + dot(pooled, w_nin_ref[512:1024])
    node_hidden = (node_pre * jax.nn.sigmoid(node_pre)).astype(BF16)
    node_unit, node_scale = normed(dot(node_hidden, w_nout_ref[...]))
    new_nodes_ref[...] = (nodes.astype(F32) + node_unit * gain_n).astype(BF16)
    new_nodes_out = pltpu.make_async_copy(new_nodes_ref, new_nodes_hbm, out_sems.at[1])
    new_nodes_out.start()
    node_cot = node_cot_ref[...].astype(F32)
    gain_grad_n = jnp.sum(node_cot * node_unit, axis=0, keepdims=True)
    back = normed_back(node_cot * gain_n, node_unit, node_scale).astype(BF16)
    big_ref[3072:3584] = dot(node_hidden, back, 0, 0).astype(BF16)
    back = dot(back, w_nout_ref[...], 1, 1).astype(BF16).astype(F32)
    back = (back * silu_slope(node_pre)).astype(BF16)
    big_ref[2048:2560] = dot(nodes, back, 0, 0).astype(BF16)
    big_ref[2560:3072] = dot(pooled, back, 0, 0).astype(BF16)
    own_grad = node_cot + dot(back, w_nin_ref[0:512], 1, 1).astype(BF16).astype(F32)
    pooled_grad = dot(back, w_nin_ref[512:1024], 1, 1).astype(BF16)
    edge_cot = edge_cot_ref[...].astype(F32)
    grad = edge_cot + dot(one_hot(down(index_ref[3:4], 384), 0, 256), pooled_grad)
    unit = unit_ref[...]
    gain_grad_e = jnp.sum(grad * unit, axis=0, keepdims=True)
    back = normed_back(grad * gain_e, unit, scale).astype(BF16)
    big_ref[1536:2048] = dot(hidden, back, 0, 0).astype(BF16)
    back = dot(back, w_eout_ref[...], 1, 1).astype(BF16).astype(F32)
    back = (back * silu_slope(pre)).astype(BF16)
    send_grad = dot(back, w_ein_ref[0:512], 1, 1).astype(BF16)
    recv_grad = dot(back, w_ein_ref[512:1024], 1, 1).astype(BF16)
    big_ref[0:512] = dot(send_rows, back, 0, 0).astype(BF16)
    big_ref[512:1024] = dot(recv_rows_ref[...], back, 0, 0).astype(BF16)
    big_ref[1024:1536] = dot(edges_ref[...], back, 0, 0).astype(BF16)
    edge_grad_ref[...] = (
        edge_cot + dot(back, w_ein_ref[1024:1536], 1, 1).astype(BF16).astype(F32)
    ).astype(BF16)
    edge_grad_out = pltpu.make_async_copy(edge_grad_ref, edge_grad_hbm, out_sems.at[2])
    edge_grad_out.start()
    senders = index_ref[1:2]
    own_grad_ref[...] = (
        own_grad
        + dot(one_hot_t(index_ref[2:3], 0, 256), recv_grad)
        + dot(one_hot_t(senders, 0, 256), send_grad)
    )
    own_grad_out = pltpu.make_async_copy(own_grad_ref, own_grad_hbm, out_sems.at[3])
    own_grad_out.start()
    rim_grad_ref[...] = dot(one_hot_t(senders, 256, 512), send_grad).astype(BF16)
    coarse_ref[...] = dot(one_hot_t(senders, 768, 1024), send_grad).astype(BF16)
    row = lax.broadcasted_iota(jnp.int32, (16, WIDTH), 0)
    gains = jnp.where(row == 0, gain_grad_e, jnp.where(row == 1, gain_grad_n, 0.0)).astype(BF16)
    x, core = place_ref[0], place_ref[1]
    for half, offsets in ((0, (0, 1, 3, 2)), (1, (0, 3, 1, 2))):
        for at, offset in enumerate(offsets):
            sides = (keep_far_ref, send_far_ref) if at >= 2 else (keep_near_ref, send_near_ref)
            for ref, other in zip(sides, (core, 1 - core)):
                block = (x ^ offset) * 2 + other
                rows = pl.ds(pl.multiple_of(block * 448 + half * 224, 32), 224)
                ref[half, at % 2, 0:224] = big_ref[rows]
                rows = pl.ds(pl.multiple_of(block * 128 + half * 64, 64), 64)
                ref[half, at % 2, 224:288] = coarse_ref[rows]
                ref[half, at % 2, 288:304] = gains
    for copy in (new_edges_out, new_nodes_out, edge_grad_out, own_grad_out):
        copy.wait()


def finish_kernel(
    factor, rim_ref, coarse_ref, own_ref, a_ref, b_ref, c_ref, d_ref, kept_ref, got_ref, out_ref, weights_ref, gains_ref, sum_ref
):
    into = one_hot_t(rim_ref[...], 0, 256)
    total = own_ref[...] + dot(into, a_ref[...]) + dot(into, b_ref[...])
    total = total + dot(into, c_ref[...]) + dot(into, d_ref[...])
    sum_ref[...] = kept_ref[...].astype(F32) + got_ref[...].astype(F32)
    weights_ref[...] = sum_ref[0:14] * factor
    gains_ref[...] = sum_ref[14:16] * factor
    at = lax.broadcasted_iota(jnp.int32, (256, 8), 0)
    coarse_into = (at == coarse_ref[...]).astype(F32)
    total = total + lax.dot_general(
        coarse_into,
        sum_ref[16:24],
        (((1,), (0,)), ((), ())),
        precision=lax.Precision.HIGHEST,
        preferred_element_type=F32,
    )
    out_ref[...] = total.astype(BF16)


def call(kernel, out, *operands, scratch=(), small=(), there=(), out_there=(), flops=0, limit=48):
    def spec(at, away):
        return pl.BlockSpec(memory_space=pltpu.SMEM if at in small else pltpu.HBM if at in away else pltpu.VMEM)

    size = sum(value.size * value.dtype.itemsize for value in operands)
    size += sum(math.prod(shape) * jnp.dtype(dtype).itemsize for shape, dtype in out)
    return pl.pallas_call(
        kernel,
        out_shape=[jax.ShapeDtypeStruct(*leaf) for leaf in out],
        in_specs=[spec(at, there) for at in range(len(operands))],
        out_specs=[pl.BlockSpec(memory_space=pltpu.HBM if at in out_there else pltpu.VMEM) for at in range(len(out))],
        scratch_shapes=list(scratch),
        compiler_params=pltpu.CompilerParams(vmem_limit_bytes=limit * 1024 * 1024),
        cost_estimate=pl.CostEstimate(flops=flops, bytes_accessed=size, transcendentals=0),
    )(*operands)


def on_device(
    node_latent,
    edge_latent,
    senders,
    receivers,
    edge_live,
    halo_list,
    coarse_list,
    edge_in_w,
    edge_out_w,
    node_in_w,
    node_out_w,
    edge_gain,
    node_gain,
    node_cot,
    edge_cot,
):
    nodes, edges = node_latent[0, 0, 0], edge_latent[0, 0, 0]
    send, recv = senders[0], receivers[0]
    rim_list, coarse_ids = halo_list[0], coarse_list[0]
    x, core, *_ = position()
    outgoing, coarse_own = call(
        outgoing_kernel,
        [((128, WIDTH), BF16), ((8, WIDTH), BF16)],
        rim_list,
        coarse_ids,
        nodes,
        flops=2 * 136 * 256 * 512,
        limit=16,
    )
    rims = [shifted(outgoing, "lat", step) for step in (1, -1)]
    slot = jnp.where(send >= 768, 768 + coarse_slot(send - 768), send)
    live_recv = jnp.where(edge_live[0] != 0, recv, -1)
    index = jnp.concatenate([slot, send, recv, live_recv, slot, slot, slot, slot], axis=0)
    pre, node_pre, recv_rows, own_rows = call(
        near_kernel,
        [((384, WIDTH), F32), ((256, WIDTH), F32), ((384, WIDTH), BF16), ((384, WIDTH), BF16)],
        index,
        nodes,
        edges,
        edge_in_w,
        node_in_w,
        scratch=[
            pltpu.VMEM((256, WIDTH), BF16),
            pltpu.VMEM((384, WIDTH), BF16),
            pltpu.VMEM((1536, WIDTH), BF16),
            pltpu.VMEM((512, WIDTH), BF16),
            pltpu.SemaphoreType.DMA((4,)),
        ],
        there=(1, 2, 3, 4),
        flops=2 * 384 * 2048 * 512,
        limit=24,
    )
    rows = doubled(coarse_own, ("y", 1), ("ring", 1), ("ring", -1))
    rows, *rims = lax.optimization_barrier((rows, *rims))
    rows = doubled(rows, ("ring", 3))
    rows, outgoing, pre, node_pre, recv_rows, own_rows = lax.optimization_barrier(
        (rows, outgoing, pre, node_pre, recv_rows, own_rows)
    )
    top, low = doubled(rows[:64], ("x", 1)), doubled(rows[64:], ("x", 3))
    rims += [from_behind(outgoing, "lon", step) for step in (1, -1)]
    top, low, *rims = lax.optimization_barrier((top, low, *rims))
    gathered = [doubled(top, ("x", 3)), doubled(low, ("x", 1))]
    gathered += [exchange(rows, "core") for rows in gathered]
    place = jnp.stack([x, core]).astype(jnp.int32)
    new_nodes, new_edges, edge_grad, own_grad, rim_grad, *units = call(
        layer_kernel,
        [
            ((256, WIDTH), BF16),
            ((384, WIDTH), BF16),
            ((384, WIDTH), BF16),
            ((256, WIDTH), F32),
            ((512, WIDTH), BF16),
            ((2, 2, UNIT, WIDTH), BF16),
            ((2, 2, UNIT, WIDTH), BF16),
            ((2, 2, UNIT, WIDTH), BF16),
            ((2, 2, UNIT, WIDTH), BF16),
        ],
        place,
        index,
        pre,
        node_pre,
        recv_rows,
        own_rows,
        edges,
        nodes,
        *rims,
        *gathered,
        edge_in_w,
        edge_out_w,
        node_in_w,
        node_out_w,
        edge_gain[None],
        node_gain[None],
        node_cot[0, 0, 0],
        edge_cot[0, 0, 0],
        scratch=[
            pltpu.VMEM((3584, WIDTH), BF16),
            pltpu.VMEM((1024, WIDTH), BF16),
            pltpu.VMEM((384, WIDTH), F32),
            pltpu.VMEM((384, WIDTH), BF16),
            pltpu.VMEM((256, WIDTH), BF16),
            pltpu.VMEM((1536, WIDTH), BF16),
            pltpu.VMEM((512, WIDTH), BF16),
            pltpu.VMEM((1024, WIDTH), BF16),
            pltpu.VMEM((512, WIDTH), BF16),
            pltpu.VMEM((256, WIDTH), BF16),
            pltpu.VMEM((384, WIDTH), BF16),
            pltpu.VMEM((256, WIDTH), BF16),
            pltpu.VMEM((384, WIDTH), BF16),
            pltpu.VMEM((384, WIDTH), BF16),
            pltpu.VMEM((256, WIDTH), F32),
            pltpu.SemaphoreType.DMA((8,)),
            pltpu.SemaphoreType.DMA((4,)),
        ],
        small=(0,),
        there=(6, 7, 16, 17, 18, 19, 22, 23),
        out_there=(0, 1, 2, 3),
        flops=2 * 384 * 512 * 10000,
    )
    kept, got, back = reduce_all(*units, rim_grad)
    devices = lax.axis_size("lat") * lax.axis_size("lon") * lax.axis_size("dp")
    node_grad, weight_share, gain_grad = call(
        functools.partial(finish_kernel, 1.0 / math.sqrt(384 * devices)),
        [((256, WIDTH), BF16), ((14, WIDTH), F32), ((2, WIDTH), F32)],
        rim_list,
        coarse_ids,
        own_grad,
        *back,
        kept,
        got,
        scratch=[pltpu.VMEM((24, WIDTH), F32)],
        flops=2 * 512 * 256 * 512,
        limit=16,
    )
    wrap = (None, None, None)
    return (
        new_nodes[wrap],
        new_edges[wrap],
        node_grad[wrap],
        edge_grad[wrap],
        weight_share.reshape(-1),
        gain_grad,
    )


def solution(mesh):
    placed = (
        P("dp", "lat", "lon", None, None),
        P("dp", "lat", "lon", None, None),
        P("lat", "lon", None),
        P("lat", "lon", None),
        P("lat", "lon", None),
        P("lat", "lon", None),
        P("lat", "lon", None),
        P(),
        P(),
        P(),
        P(),
        P(),
        P(),
        P("dp", "lat", "lon", None, None),
        P("dp", "lat", "lon", None, None),
    )
    return jax.shard_map(
        on_device,
        mesh=mesh,
        in_specs=placed,
        out_specs=(
            P("dp", "lat", "lon", None, None),
            P("dp", "lat", "lon", None, None),
            P("dp", "lat", "lon", None, None),
            P("dp", "lat", "lon", None, None),
            P(("lat", "lon", "dp")),
            P(),
        ),
        check_vma=False,
    )
```

time: 1300 us -> 135 us (0.10)
  waiting for transfers between devices: 1080 us -> 54.6 us
  blocking collectives: 79.1 us -> 0 us
  other arithmetic: 67.6 us -> 5 us
  starting transfers between devices: 16.7 us -> 46.6 us
  Pallas kernels: 0 us -> 16.4 us
  between operations: 14.6 us -> 1.13 us
    reduce_scatter x1 -> x0, waiting for transfers between devices: 566 us -> none  [on_device(): lax.psum_scatter(coarse_grad_all, ('lat', 'lon'), scatter_dimension=0, ti...]
    all_gather x1 -> x0, waiting for transfers between devices: 345 us -> none  [on_device(): coarse_all = lax.all_gather(coarse_own, ('lat', 'lon'), axis=0, tiled=True)]
    unnamed x4 -> x0, waiting for transfers between devices: 169 us -> none
    psum x1 -> x0, blocking collectives: 79.1 us -> none  [on_device(): lax.psum((grads[7], grads[8]), ('lat', 'lon', 'dp'))]
    ppermute x0 -> x21, waiting for transfers between devices: none -> 46.6 us  [exchange(): return lax.ppermute(value, AXES, pairs)]
    ppermute x0 -> x21, starting transfers between devices: none -> 33 us  [exchange(): return lax.ppermute(value, AXES, pairs)]
    concatenate x2 -> x8, other arithmetic: 28.6 us -> 0.09 us  [the longest x6 0.04 us: doubled(): rows = jnp.concatenate([rows, exchange(rows, kind, amount)], axis=0)]
    pallas_call x0 -> x4, Pallas kernels: none -> 16.4 us  [call(): pl.pallas_call(kernel, out_shape=[jax.ShapeDtypeStruct(*leaf) for leaf in...]
  transfers between devices with their start and end apart: 11 -> 29, of which waited for: 3 -> 17; matrix products, arithmetic and copies ran while one was open for 3% -> 3% of each run, Pallas kernels for 0% -> 2%
where the time goes in v1:
time: 135 us; the launch traced here: 133 us
  waiting for transfers between devices  54.6 us (40%)
  starting transfers between devices  46.6 us (35%)
  Pallas kernels  16.4 us (12%)
  local copies, waits for them, and re-layouts  9.68 us (7%)
  other arithmetic  5 us (4%)
    ppermute x21, waiting for transfers between devices, exchange(): return lax.ppermute(value, AXES, pairs)  46.6 us
    ppermute x21, starting transfers between devices, exchange(): return lax.ppermute(value, AXES, pairs)  33 us
    pallas_call x4, Pallas kernels, call(): pl.pallas_call(kernel, out_shape=[jax.ShapeDtypeStruct(*leaf) for leaf in...  16.4 us
    unnamed x44, local copies, waits for them, and re-layouts  8.01 us
    ppermute x4, waiting for transfers between devices, from_behind(): return lax.ppermute(value, axis, pairs)  7.09 us
    ppermute x4, starting transfers between devices, shifted(): return lax.ppermute(block, axis, route)  6.91 us
    ppermute x4, starting transfers between devices, from_behind(): return lax.ppermute(value, axis, pairs)  6.67 us
    convert_element_type x7, other arithmetic, plus(): return total.astype(BF16)  3.99 us
  transfers between devices with their start and end apart: 29, of which 17 were waited for; matrix products, arithmetic and copies ran while one was open for 3% of the time, Pallas kernels for 2%

profile of v1, /device:TPU:16, one launch (start us, length us, event | category | flops | bytes accessed | tf_op | source)
XLA Modules:
  0.0 133.4 jit_solution(10485107179314778830)
XLA Ops:
  0.6 0.9 copy-done.1
  1.6 0.7 copy-done.7
  3.1 1.4 %collective-permute-start = (bf16[8,512]{1,0:T(8,128)(2,1)S(1)}, bf16[8,512]{1,0:T(8,128)(2,1)S(1)}, u32[]{:S(2)}, u32[]{:S(2)}) collective-permute-start(bf16[8,512]{1,0:T(8,128)(2,1)S(1)} %get-tuple-element.49), channel_id=1, source_target_pairs={{0,2},{1,3},{2,0},{3,1},{4,6},{5,7},{6,4},{7,5},{8,10},{9,11},{10,... | collective-permute-start | bytes 24584 | tf_op jit(solution)/shard_map/ppermute | solution.py:49
  4.5 2.4 %collective-permute-done = bf16[8,512]{1,0:T(8,128)(2,1)S(1)} collective-permute-done((bf16[8,512]{1,0:T(8,128)(2,1)S(1)}, bf16[8,512]{1,0:T(8,128)(2,1)S(1)}, u32[]{:S(2)}, u32[]{:S(2)}) %collective-permute-start) | collective-permute-done | bytes 8224 | tf_op jit(solution)/shard_map/ppermute | solution.py:49
  6.9 1.9 %collective-permute-start.1 = (bf16[16,512]{1,0:T(8,128)(2,1)S(1)}, bf16[16,512]{1,0:T(8,128)(2,1)S(1)}, u32[]{:S(2)}, u32[]{:S(2)}) collective-permute-start(bf16[16,512]{1,0:T(8,128)(2,1)S(1)} %pad_maximum_fusion.7), channel_id=1, source_target_pairs={{0,4},{1,5},{2,6},{3,7},{4,0},{5,1},{6,2},{7,3},{8,12},{9,13},{10,... | collective-permute-start | bytes 49160 | tf_op jit(solution)/shard_map/ppermute | solution.py:49
  8.8 1.3 collective-permute-start.3
  10.1 1.3 collective-permute-start.4
  11.4 5.1 %collective-permute-start.2 = (bf16[32,512]{1,0:T(8,128)(2,1)S(1)}, bf16[32,512]{1,0:T(8,128)(2,1)S(1)}, u32[]{:S(2)}, u32[]{:S(2)}) collective-permute-start(bf16[32,512]{1,0:T(8,128)(2,1)S(1)} %pad_maximum_fusion.6), channel_id=1, source_target_pairs={{0,28},{1,29},{2,30},{3,31},{4,8},{5,9},{6,10},{7,11},{8,4},{9,5},... | collective-permute-start | bytes 98312 | tf_op jit(solution)/shard_map/ppermute | solution.py:49
  16.5 0.7 compare_select_fusion
  17.2 0.7 concatenate.44.index_ref
  18.4 2.1 %collective-permute-start.5 = (bf16[64,512]{1,0:T(8,128)(2,1)S(1)}, bf16[64,512]{1,0:T(8,128)(2,1)S(1)}, u32[]{:S(2)}, u32[]{:S(2)}) collective-permute-start(bf16[64,512]{1,0:T(8,128)(2,1)S(1)} %pad_maximum_fusion.5), channel_id=1, source_target_pairs={{0,12},{1,13},{2,14},{3,15},{4,24},{5,25},{6,26},{7,27},{8,20},{9,... | collective-permute-start | bytes 196616 | tf_op jit(solution)/shard_map/ppermute | solution.py:49
  20.5 1.4 %copy-done = bf16[1536,512]{1,0:T(8,128)(2,1)S(1)} copy-done((bf16[1536,512]{1,0:T(8,128)(2,1)S(1)}, bf16[1536,512]{1,0:T(8,128)(2,1)}, u32[]{:S(2)}) %copy-start) | copy-done | bytes 1572888
  21.9 0.9 copy-done.2
  22.8 1.2 copy-done.4
  24.1 1.0 copy-done.5
  25.1 2.0 %shard_map.191 = (f32[384,512]{1,0:T(8,128)S(1)}, f32[256,512]{1,0:T(8,128)S(1)}, bf16[384,512]{1,0:T(8,128)(2,1)S(1)}, bf16[384,512]{1,0:T(8,128)(2,1)S(1)}) custom-call(s32[8,384]{1,0:T(8,128)S(1)} %concatenate.44.index_ref, bf16[256,512]{1,0:T(8,128)(2,1)S(1)} %bitcast.75, bf16[384,512]{1,0:T(8,128)(2,1)S(1)} %bitcast.77, bf16[1536,512]{1,0:T(8,128)(2,1)S(1)} %copy-done, ...), custom_call_target="tpu_custom_call" | custom-call | flops 805306368 | bytes 5386240 | tf_op jit(solution)/shard_map/pallas_call | solution.py:398
  27.2 5.7 %collective-permute-start.7 = (bf16[64,512]{1,0:T(8,128)(2,1)S(1)}, bf16[64,512]{1,0:T(8,128)(2,1)S(1)}, u32[]{:S(2)}, u32[]{:S(2)}) collective-permute-start(bf16[64,512]{1,0:T(8,128)(2,1)S(1)} %get-tuple-element.102), channel_id=1, source_target_pairs={{0,192},{1,193},{2,194},{3,195},{4,196},{5,197},{6,198},{7,199},{8... | collective-permute-start | bytes 196616 | tf_op jit(solution)/shard_map/ppermute | solution.py:49
  32.9 1.3 collective-permute-start.8
  34.2 2.9 %collective-permute-start.9 = (bf16[128,512]{1,0:T(8,128)(2,1)S(1)}, bf16[128,512]{1,0:T(8,128)(2,1)S(1)}, u32[]{:S(2)}, u32[]{:S(2)}) collective-permute-start(bf16[128,512]{1,0:T(8,128)(2,1)S(1)} %get-tuple-element.63), channel_id=1, source_target_pairs={{0,30},{2,0},{4,2},{6,4},{8,6},{10,8},{12,10},{14,12},{16,14},{18,... | collective-permute-start | bytes 393224 | tf_op jit(solution)/shard_map/ppermute | solution.py:27
  37.3 4.0 %collective-permute-done.6 = bf16[64,512]{1,0:T(8,128)(2,1)S(1)} collective-permute-done((bf16[64,512]{1,0:T(8,128)(2,1)S(1)}, bf16[64,512]{1,0:T(8,128)(2,1)S(1)}, u32[]{:S(2)}, u32[]{:S(2)}) %collective-permute-start.6) | collective-permute-done | bytes 65568 | tf_op jit(solution)/shard_map/ppermute | solution.py:49
  41.8 1.5 %collective-permute-start.10 = (bf16[128,512]{1,0:T(8,128)(2,1)S(1)}, bf16[128,512]{1,0:T(8,128)(2,1)S(1)}, u32[]{:S(2)}, u32[]{:S(2)}) collective-permute-start(bf16[128,512]{1,0:T(8,128)(2,1)S(1)} %pad_maximum_fusion.2), channel_id=1, source_target_pairs={{0,192},{1,193},{2,194},{3,195},{4,196},{5,197},{6,198},{7,199},{8... | collective-permute-start | bytes 393224 | tf_op jit(solution)/shard_map/ppermute | solution.py:49
  43.3 3.1 %collective-permute-done.11 = bf16[128,512]{1,0:T(8,128)(2,1)S(1)} collective-permute-done((bf16[128,512]{1,0:T(8,128)(2,1)S(1)}, bf16[128,512]{1,0:T(8,128)(2,1)S(1)}, u32[]{:S(2)}, u32[]{:S(2)}) %collective-permute-start.11) | collective-permute-done | bytes 131104 | tf_op jit(solution)/shard_map/ppermute | solution.py:49
  46.5 1.5 %collective-permute-done.10 = bf16[128,512]{1,0:T(8,128)(2,1)S(1)} collective-permute-done((bf16[128,512]{1,0:T(8,128)(2,1)S(1)}, bf16[128,512]{1,0:T(8,128)(2,1)S(1)}, u32[]{:S(2)}, u32[]{:S(2)}) %collective-permute-start.10) | collective-permute-done | bytes 131104 | tf_op jit(solution)/shard_map/ppermute | solution.py:49
  48.4 1.4 %collective-permute-done.12.far_top_ref = bf16[256,512]{1,0:T(8,128)(2,1)S(1)} collective-permute-done((bf16[256,512]{1,0:T(8,128)(2,1)S(1)}, bf16[256,512]{1,0:T(8,128)(2,1)S(1)}, u32[]{:S(2)}, u32[]{:S(2)}) %collective-permute-start.12) | collective-permute-done | bytes 262176 | tf_op jit(solution)/shard_map/ppermute | solution.py:49
  49.9 12.6 %shard_map.192 = (bf16[256,512]{1,0:T(8,128)(2,1)}, bf16[384,512]{1,0:T(8,128)(2,1)}, bf16[384,512]{1,0:T(8,128)(2,1)}, f32[256,512]{1,0:T(8,128)S(1)}, bf16[512...) custom-call(s32[2]{0:T(128)S(1)} %pad_add_fusion.place_ref, ...), custom_call_target="tpu_custom_call" | custom-call | flops 3932160000 | bytes 15745032 | tf_op jit(solution)/shard_map/pallas_call | solution.py:398
  63.2 2.6 %collective-permute-done.15 = bf16[2,2,304,512]{3,2,1,0:T(8,128)(2,1)S(1)} collective-permute-done((bf16[2,2,304,512]{3,2,1,0:T(8,128)(2,1)}, bf16[2,2,304,512]{3,2,1,0:T(8,128)(2,1)S(1)}, u32[]{:S(2)}, u32[]{:S(2)}) %collective-permute-start.15) | collective-permute-done | bytes 1245216 | tf_op jit(solution)/shard_map/ppermute | solution.py:49
  65.8 1.7 %fusion.1 = (bf16[2,304,512]{2,1,0:T(8,128)(2,1)S(1)}, bf16[2,304,512]{2,1,0:T(8,128)(2,1)S(1)}) fusion(bf16[2,2,304,512]{3,2,1,0:T(8,128)(2,1)S(1)} %collective-permute-done.15, bf16[2,2,304,512]{3,2,1,0:T(8,128)(2,1)} %get-tuple-element.75), kind=kLoop, calls=%fused_computation.5 | loop fusion | flops 3112960 | bytes 3735552 | tf_op jit(solution)/shard_map/convert_element_type | solution.py:81
  67.5 1.5 %collective-permute-start.16 = (bf16[2,304,512]{2,1,0:T(8,128)(2,1)S(1)}, bf16[2,304,512]{2,1,0:T(8,128)(2,1)S(1)}, u32[]{:S(2)}, u32[]{:S(2)}) collective-permute-start(bf16[2,304,512]{2,1,0:T(8,128)(2,1)S(1)} %get-tuple-element.97), channel_id=1, source_target_pairs={{0,192},{1,193},{2,194},{3,195},{4,196},{5,197},{6,198},{7,199},{8... | collective-permute-start | bytes 1867784 | tf_op jit(solution)/shard_map/ppermute | solution.py:49
  69.1 2.5 %collective-permute-start.18 = (bf16[128,512]{1,0:T(8,128)(2,1)S(1)}, bf16[128,512]{1,0:T(8,128)(2,1)S(1)}, u32[]{:S(2)}, u32[]{:S(2)}) collective-permute-start(bf16[128,512]{1,0:T(8,128)(2,1)S(1)} %get-tuple-element.101), channel_id=1, source_target_pairs={{0,30},{2,0},{4,2},{6,4},{8,6},{10,8},{12,10},{14,12},{16,14},{18,... | collective-permute-start | bytes 393224 | tf_op jit(solution)/shard_map/ppermute | solution.py:27
  71.6 2.8 %collective-permute-done.18.c_ref = bf16[128,512]{1,0:T(8,128)(2,1)S(1)} collective-permute-done((bf16[128,512]{1,0:T(8,128)(2,1)S(1)}, bf16[128,512]{1,0:T(8,128)(2,1)S(1)}, u32[]{:S(2)}, u32[]{:S(2)}) %collective-permute-start.18) | collective-permute-done | bytes 131104 | tf_op jit(solution)/shard_map/ppermute | solution.py:27
  74.4 4.3 %collective-permute-done.19.d_ref = bf16[128,512]{1,0:T(8,128)(2,1)S(1)} collective-permute-done((bf16[128,512]{1,0:T(8,128)(2,1)S(1)}, bf16[128,512]{1,0:T(8,128)(2,1)S(1)}, u32[]{:S(2)}, u32[]{:S(2)}) %collective-permute-start.19) | collective-permute-done | bytes 131104 | tf_op jit(solution)/shard_map/ppermute | solution.py:27
  78.7 6.2 %collective-permute-done.16 = bf16[2,304,512]{2,1,0:T(8,128)(2,1)S(1)} collective-permute-done((bf16[2,304,512]{2,1,0:T(8,128)(2,1)S(1)}, bf16[2,304,512]{2,1,0:T(8,128)(2,1)S(1)}, u32[]{:S(2)}, u32[]{:S(2)}) %collective-permute-start.16) | collective-permute-done | bytes 622624 | tf_op jit(solution)/shard_map/ppermute | solution.py:49
  86.4 1.8 %collective-permute-start.21 = (bf16[304,512]{1,0:T(8,128)(2,1)S(1)}, bf16[304,512]{1,0:T(8,128)(2,1)}, u32[]{:S(2)}, u32[]{:S(2)}) collective-permute-start(bf16[304,512]{1,0:T(8,128)(2,1)S(1)} %get-tuple-element.94), channel_id=1, source_target_pairs={{0,192},{1,193},{2,194},{3,195},{4,196},{5,197},{6,198},{7,199},{8... | collective-permute-start | bytes 933896 | tf_op jit(solution)/shard_map/ppermute | solution.py:49
  88.2 6.7 %collective-permute-done.20 = bf16[304,512]{1,0:T(8,128)(2,1)S(1)} collective-permute-done((bf16[304,512]{1,0:T(8,128)(2,1)S(1)}, bf16[304,512]{1,0:T(8,128)(2,1)S(1)}, u32[]{:S(2)}, u32[]{:S(2)}) %collective-permute-start.20) | collective-permute-done | bytes 311328 | tf_op jit(solution)/shard_map/ppermute | solution.py:49
  94.9 1.3 collective-permute-done.21
  96.2 1.7 %fusion.13 = (bf16[304,512]{1,0:T(8,128)(2,1)S(1)}, bf16[304,512]{1,0:T(8,128)(2,1)S(1)}) fusion(bf16[304,512]{1,0:T(8,128)(2,1)S(1)} %collective-permute-done.20, bf16[2,2,304,512]{3,2,1,0:T(8,128)(2,1)} %copy-done.18, bf16[2,304,512]{2,1,0:T(8,128)(2,1)} %copy-done.19, bf16[2,2,304,512]{3,2,1,0:T(8,128)(2,1)S(1)} %copy-done.17, ...), kind=kLoop, calls=%fused_computation.21 | loop fusion | flops 3424256 | bytes 3112960 | tf_op jit(solution)/shard_map/convert_element_type | solution.py:81
  98.5 6.5 %collective-permute-done.22 = bf16[8,2,16,512]{3,2,1,0:T(8,128)(2,1)S(1)} collective-permute-done((bf16[8,2,16,512]{3,2,1,0:T(8,128)(2,1)S(1)}, bf16[8,2,16,512]{3,2,1,0:T(8,128)(2,1)S(1)}, u32[]{:S(2)}, u32[]{:S(2)}) %collective-permute-start.22) | collective-permute-done | bytes 262176 | tf_op jit(solution)/shard_map/ppermute | solution.py:49
  105.2 2.0 %collective-permute-start.23 = (bf16[8,24,512]{2,1,0:T(8,128)(2,1)S(1)}, bf16[8,24,512]{2,1,0:T(8,128)(2,1)S(1)}, u32[]{:S(2)}, u32[]{:S(2)}) collective-permute-start(bf16[8,24,512]{2,1,0:T(8,128)(2,1)S(1)} %fusion.23), channel_id=1, source_target_pairs={{0,2},{1,3},{2,0},{3,1},{4,6},{5,7},{6,4},{7,5},{8,10},{9,11},{10,... | collective-permute-start | bytes 589832 | tf_op jit(solution)/shard_map/ppermute | solution.py:49
  107.2 1.3 collective-permute-start.24
  108.5 3.0 %collective-permute-start.25 = (bf16[128,512]{1,0:T(8,128)(2,1)S(1)}, bf16[128,512]{1,0:T(8,128)(2,1)S(1)}, u32[]{:S(2)}, u32[]{:S(2)}) collective-permute-start(bf16[128,512]{1,0:T(8,128)(2,1)S(1)} %get-tuple-element.98), channel_id=1, source_target_pairs={{0,32},{32,64},{64,96},{96,128},{128,160},{160,192},{192,224},{1,3... | collective-permute-start | bytes 393224 | tf_op jit(solution)/shard_map/ppermute | solution.py:21
  111.7 0.9 collective-permute-done.25.b_ref
  112.5 1.7 %collective-permute-start.26 = (bf16[2,2,24,512]{3,2,1,0:T(8,128)(2,1)S(1)}, bf16[2,2,24,512]{3,2,1,0:T(8,128)(2,1)S(1)}, u32[]{:S(2)}, u32[]{:S(2)}) collective-permute-start(bf16[2,2,24,512]{3,2,1,0:T(8,128)(2,1)S(1)} %dynamic-slice_bitcast_fusion), channel_id=1, source_target_pairs={{0,4},{1,5},{2,6},{3,7},{4,0},{5,1},{6,2},{7,3},{8,12},{9,13},{10,... | collective-permute-start | bytes 294920 | tf_op jit(solution)/shard_map/ppermute | solution.py:49
  114.3 3.9 %collective-permute-done.26 = bf16[2,2,24,512]{3,2,1,0:T(8,128)(2,1)S(1)} collective-permute-done((bf16[2,2,24,512]{3,2,1,0:T(8,128)(2,1)S(1)}, bf16[2,2,24,512]{3,2,1,0:T(8,128)(2,1)S(1)}, u32[]{:S(2)}, u32[]{:S(2)}) %collective-permute-start.26) | collective-permute-done | bytes 98336 | tf_op jit(solution)/shard_map/ppermute | solution.py:49
  118.3 2.7 %collective-permute-start.27 = (bf16[2,24,512]{2,1,0:T(8,128)(2,1)S(1)}, bf16[2,24,512]{2,1,0:T(8,128)(2,1)S(1)}, u32[]{:S(2)}, u32[]{:S(2)}) collective-permute-start(bf16[2,24,512]{2,1,0:T(8,128)(2,1)S(1)} %dynamic-slice_bitcast_fusion.1), channel_id=1, source_target_pairs={{0,8},{1,9},{2,10},{3,11},{4,12},{5,13},{6,14},{7,15},{8,0},{9,1},... | collective-permute-start | bytes 147464 | tf_op jit(solution)/shard_map/ppermute | solution.py:49
  120.9 2.4 %collective-permute-done.27 = bf16[2,24,512]{2,1,0:T(8,128)(2,1)S(1)} collective-permute-done((bf16[2,24,512]{2,1,0:T(8,128)(2,1)S(1)}, bf16[2,24,512]{2,1,0:T(8,128)(2,1)S(1)}, u32[]{:S(2)}, u32[]{:S(2)}) %collective-permute-start.27) | collective-permute-done | bytes 49184 | tf_op jit(solution)/shard_map/ppermute | solution.py:49
  123.4 3.8 %collective-permute-start.28 = (bf16[24,512]{1,0:T(8,128)(2,1)S(1)}, bf16[24,512]{1,0:T(8,128)(2,1)S(1)}, u32[]{:S(2)}, u32[]{:S(2)}) collective-permute-start(bf16[24,512]{1,0:T(8,128)(2,1)S(1)} %get-tuple-element.104), channel_id=1, source_target_pairs={{0,16},{1,17},{2,18},{3,19},{4,20},{5,21},{6,22},{7,23},{8,24},{9,... | collective-permute-start | bytes 73736 | tf_op jit(solution)/shard_map/ppermute | solution.py:49
  127.2 4.0 %collective-permute-done.28.got_ref = bf16[24,512]{1,0:T(8,128)(2,1)S(1)} collective-permute-done((bf16[24,512]{1,0:T(8,128)(2,1)S(1)}, bf16[24,512]{1,0:T(8,128)(2,1)S(1)}, u32[]{:S(2)}, u32[]{:S(2)}) %collective-permute-start.28) | collective-permute-done | bytes 24608 | tf_op jit(solution)/shard_map/ppermute | solution.py:49
  131.2 1.5 %shard_map.193 = (bf16[256,512]{1,0:T(8,128)(2,1)}, f32[14,512]{1,0:T(8,128)S(1)}, f32[2,512]{1,0:T(2,128)}) custom-call(s32[1,128]{1,0:T(1,128)S(1)} %bitcast.80, s32[1,8]{1,0:T(1,128)S(1)} %bitcast.82, f32[256,512]{1,0:T(8,128)S(1)} %get-tuple-element.72.own_ref, bf16[128,512]{1,0:T(8,128)(2,1)S(1)} %collective-permute-done.24.a_ref, ...), custom_call_target="tpu_custom_call" | custom-call | flops 134217728 | bytes 1393184 | tf_op jit(solution)/shard_map/pallas_call | solution.py:398
  (94 shorter events, 6.0 us)
Async XLA Ops:
  0.6 1.0 copy-start.1
  3.1 3.7 %collective-permute-start = (bf16[8,512]{1,0:T(8,128)(2,1)S(1)}, bf16[8,512]{1,0:T(8,128)(2,1)S(1)}, u32[]{:S(2)}, u32[]{:S(2)}) collective-permute-start(bf16[8,512]{1,0:T(8,128)(2,1)S(1)} %get-tuple-element.49), channel_id=1, source_target_pairs={{0,2},{1,3},{2,0},{3,1},{4,6},{5,7},{6,4},{7,5},{8,10},{9,11},{10,... | collective-permute-start | bytes 24584 | tf_op jit(solution)/shard_map/ppermute | solution.py:49
  6.9 4.5 %collective-permute-start.1 = (bf16[16,512]{1,0:T(8,128)(2,1)S(1)}, bf16[16,512]{1,0:T(8,128)(2,1)S(1)}, u32[]{:S(2)}, u32[]{:S(2)}) collective-permute-start(bf16[16,512]{1,0:T(8,128)(2,1)S(1)} %pad_maximum_fusion.7), channel_id=1, source_target_pairs={{0,4},{1,5},{2,6},{3,7},{4,0},{5,1},{6,2},{7,3},{8,12},{9,13},{10,... | collective-permute-start | bytes 49160 | tf_op jit(solution)/shard_map/ppermute | solution.py:49
  8.8 9.6 %collective-permute-start.3 = (bf16[128,512]{1,0:T(8,128)(2,1)S(1)}, bf16[128,512]{1,0:T(8,128)(2,1)S(1)}, u32[]{:S(2)}, u32[]{:S(2)}) collective-permute-start(bf16[128,512]{1,0:T(8,128)(2,1)S(1)} %get-tuple-element.63), channel_id=1, source_target_pairs={{0,32},{32,64},{64,96},{96,128},{128,160},{160,192},{192,224},{1,3... | collective-permute-start | bytes 393224 | tf_op jit(solution)/shard_map/ppermute | solution.py:21
  10.1 8.3 %collective-permute-start.4 = (bf16[128,512]{1,0:T(8,128)(2,1)S(1)}, bf16[128,512]{1,0:T(8,128)(2,1)S(1)}, u32[]{:S(2)}, u32[]{:S(2)}) collective-permute-start(bf16[128,512]{1,0:T(8,128)(2,1)S(1)} %get-tuple-element.63), channel_id=1, source_target_pairs={{32,0},{64,32},{96,64},{128,96},{160,128},{192,160},{224,192},{33,... | collective-permute-start | bytes 393224 | tf_op jit(solution)/shard_map/ppermute | solution.py:21
  11.4 6.9 %collective-permute-start.2 = (bf16[32,512]{1,0:T(8,128)(2,1)S(1)}, bf16[32,512]{1,0:T(8,128)(2,1)S(1)}, u32[]{:S(2)}, u32[]{:S(2)}) collective-permute-start(bf16[32,512]{1,0:T(8,128)(2,1)S(1)} %pad_maximum_fusion.6), channel_id=1, source_target_pairs={{0,28},{1,29},{2,30},{3,31},{4,8},{5,9},{6,10},{7,11},{8,4},{9,5},... | collective-permute-start | bytes 98312 | tf_op jit(solution)/shard_map/ppermute | solution.py:49
  18.4 8.8 %collective-permute-start.5 = (bf16[64,512]{1,0:T(8,128)(2,1)S(1)}, bf16[64,512]{1,0:T(8,128)(2,1)S(1)}, u32[]{:S(2)}, u32[]{:S(2)}) collective-permute-start(bf16[64,512]{1,0:T(8,128)(2,1)S(1)} %pad_maximum_fusion.5), channel_id=1, source_target_pairs={{0,12},{1,13},{2,14},{3,15},{4,24},{5,25},{6,26},{7,27},{8,20},{9,... | collective-permute-start | bytes 196616 | tf_op jit(solution)/shard_map/ppermute | solution.py:49
  20.5 1.4 %copy-start = (bf16[1536,512]{1,0:T(8,128)(2,1)S(1)}, bf16[1536,512]{1,0:T(8,128)(2,1)}, u32[]{:S(2)}) copy-start(bf16[1536,512]{1,0:T(8,128)(2,1)} %w_ein_hbm.3) | copy-start | bytes 4718596
  21.9 0.9 copy-start.2
  22.8 1.2 copy-start.4
  24.1 1.0 copy-start.5
  27.1 22.8 %copy-start.11 = (f32[384,512]{1,0:T(8,128)}, f32[384,512]{1,0:T(8,128)S(1)}, u32[]{:S(2)}) copy-start(f32[384,512]{1,0:T(8,128)S(1)} %get-tuple-element.56.pre_ref) | copy-start | bytes 2359300
  27.1 22.8 %copy-start.3 = (bf16[1,1,1,256,512]{4,3,2,1,0:T(8,128)(2,1)S(1)}, bf16[1,1,1,256,512]{4,3,2,1,0:T(8,128)(2,1)}, u32[]{:S(2)}) copy-start(bf16[1,1,1,256,512]{4,3,2,1,0:T(8,128)(2,1)} %param.15) | copy-start | bytes 786436
  27.1 22.8 %copy-start.6 = (bf16[1,1,1,384,512]{4,3,2,1,0:T(8,128)(2,1)S(1)}, bf16[1,1,1,384,512]{4,3,2,1,0:T(8,128)(2,1)}, u32[]{:S(2)}) copy-start(bf16[1,1,1,384,512]{4,3,2,1,0:T(8,128)(2,1)} %param.16) | copy-start | bytes 1179652
  27.1 22.8 %copy-start.12 = (bf16[512,512]{1,0:T(8,128)(2,1)S(1)}, bf16[512,512]{1,0:T(8,128)(2,1)}, u32[]{:S(2)}) copy-start(bf16[512,512]{1,0:T(8,128)(2,1)} %w_eout_hbm.1) | copy-start | bytes 1572868
  27.1 22.8 %copy-start.13 = (bf16[1,1,1,384,512]{4,3,2,1,0:T(8,128)(2,1)S(1)}, bf16[1,1,1,384,512]{4,3,2,1,0:T(8,128)(2,1)}, u32[]{:S(2)}) copy-start(bf16[1,1,1,384,512]{4,3,2,1,0:T(8,128)(2,1)} %param.29) | copy-start | bytes 1179652
  27.1 22.8 %copy-start.14 = (bf16[1,1,1,256,512]{4,3,2,1,0:T(8,128)(2,1)S(1)}, bf16[1,1,1,256,512]{4,3,2,1,0:T(8,128)(2,1)}, u32[]{:S(2)}) copy-start(bf16[1,1,1,256,512]{4,3,2,1,0:T(8,128)(2,1)} %param.28) | copy-start | bytes 786436
  27.1 22.8 %copy-start.15 = (f32[512]{0:T(512)S(1)}, f32[512]{0:T(512)}, u32[]{:S(2)}) copy-start(f32[512]{0:T(512)} %param.26) | copy-start | bytes 6148
  27.1 22.8 %copy-start.16 = (f32[512]{0:T(512)S(1)}, f32[512]{0:T(512)}, u32[]{:S(2)}) copy-start(f32[512]{0:T(512)} %param.27) | copy-start | bytes 6148
  27.2 10.1 %collective-permute-start.7 = (bf16[64,512]{1,0:T(8,128)(2,1)S(1)}, bf16[64,512]{1,0:T(8,128)(2,1)S(1)}, u32[]{:S(2)}, u32[]{:S(2)}) collective-permute-start(bf16[64,512]{1,0:T(8,128)(2,1)S(1)} %get-tuple-element.102), channel_id=1, source_target_pairs={{0,192},{1,193},{2,194},{3,195},{4,196},{5,197},{6,198},{7,199},{8... | collective-permute-start | bytes 196616 | tf_op jit(solution)/shard_map/ppermute | solution.py:49
  32.9 8.4 %collective-permute-start.8 = (bf16[128,512]{1,0:T(8,128)(2,1)S(1)}, bf16[128,512]{1,0:T(8,128)(2,1)S(1)}, u32[]{:S(2)}, u32[]{:S(2)}) collective-permute-start(bf16[128,512]{1,0:T(8,128)(2,1)S(1)} %get-tuple-element.63), channel_id=1, source_target_pairs={{0,2},{2,4},{4,6},{6,8},{8,10},{10,12},{12,14},{14,16},{16,18},{18... | collective-permute-start | bytes 393224 | tf_op jit(solution)/shard_map/ppermute | solution.py:27
  34.2 7.1 %collective-permute-start.9 = (bf16[128,512]{1,0:T(8,128)(2,1)S(1)}, bf16[128,512]{1,0:T(8,128)(2,1)S(1)}, u32[]{:S(2)}, u32[]{:S(2)}) collective-permute-start(bf16[128,512]{1,0:T(8,128)(2,1)S(1)} %get-tuple-element.63), channel_id=1, source_target_pairs={{0,30},{2,0},{4,2},{6,4},{8,6},{10,8},{12,10},{14,12},{16,14},{18,... | collective-permute-start | bytes 393224 | tf_op jit(solution)/shard_map/ppermute | solution.py:27
  37.1 4.3 %collective-permute-start.6 = (bf16[64,512]{1,0:T(8,128)(2,1)S(1)}, bf16[64,512]{1,0:T(8,128)(2,1)S(1)}, u32[]{:S(2)}, u32[]{:S(2)}) collective-permute-start(bf16[64,512]{1,0:T(8,128)(2,1)S(1)} %get-tuple-element.103), channel_id=1, source_target_pairs={{0,64},{1,65},{2,66},{3,67},{4,68},{5,69},{6,70},{7,71},{8,72},{9,... | collective-permute-start | bytes 196616 | tf_op jit(solution)/shard_map/ppermute | solution.py:49
  41.4 5.1 %collective-permute-start.11 = (bf16[128,512]{1,0:T(8,128)(2,1)S(1)}, bf16[128,512]{1,0:T(8,128)(2,1)S(1)}, u32[]{:S(2)}, u32[]{:S(2)}) collective-permute-start(bf16[128,512]{1,0:T(8,128)(2,1)S(1)} %pad_maximum_fusion.3), channel_id=1, source_target_pairs={{0,64},{1,65},{2,66},{3,67},{4,68},{5,69},{6,70},{7,71},{8,72},{9,... | collective-permute-start | bytes 393224 | tf_op jit(solution)/shard_map/ppermute | solution.py:49
  41.8 6.3 %collective-permute-start.10 = (bf16[128,512]{1,0:T(8,128)(2,1)S(1)}, bf16[128,512]{1,0:T(8,128)(2,1)S(1)}, u32[]{:S(2)}, u32[]{:S(2)}) collective-permute-start(bf16[128,512]{1,0:T(8,128)(2,1)S(1)} %pad_maximum_fusion.2), channel_id=1, source_target_pairs={{0,192},{1,193},{2,194},{3,195},{4,196},{5,197},{6,198},{7,199},{8... | collective-permute-start | bytes 393224 | tf_op jit(solution)/shard_map/ppermute | solution.py:49
  46.4 2.0 %collective-permute-start.13 = (bf16[256,512]{1,0:T(8,128)(2,1)S(1)}, bf16[256,512]{1,0:T(8,128)(2,1)S(1)}, u32[]{:S(2)}, u32[]{:S(2)}) collective-permute-start(bf16[256,512]{1,0:T(8,128)(2,1)S(1)} %constant_dynamic-update-slice_fusion.2.near_low_ref), channel_id=1, source_target_pairs={{0,32},{1,33},{2,34},{3,35},{4,36},{5,37},{6,38},{7,39},{8,40},{9,... | collective-permute-start | bytes 786440 | tf_op jit(solution)/shard_map/ppermute | solution.py:49
  48.1 1.8 %collective-permute-start.12 = (bf16[256,512]{1,0:T(8,128)(2,1)S(1)}, bf16[256,512]{1,0:T(8,128)(2,1)S(1)}, u32[]{:S(2)}, u32[]{:S(2)}) collective-permute-start(bf16[256,512]{1,0:T(8,128)(2,1)S(1)} %constant_dynamic-update-slice_fusion.near_top_ref), channel_id=1, source_target_pairs={{0,32},{1,33},{2,34},{3,35},{4,36},{5,37},{6,38},{7,39},{8,40},{9,... | collective-permute-start | bytes 786440 | tf_op jit(solution)/shard_map/ppermute | solution.py:49
  62.6 3.2 %collective-permute-start.15 = (bf16[2,2,304,512]{3,2,1,0:T(8,128)(2,1)}, bf16[2,2,304,512]{3,2,1,0:T(8,128)(2,1)S(1)}, u32[]{:S(2)}, u32[]{:S(2)}) collective-permute-start(bf16[2,2,304,512]{3,2,1,0:T(8,128)(2,1)} %get-tuple-element.76), channel_id=1, source_target_pairs={{0,32},{1,33},{2,34},{3,35},{4,36},{5,37},{6,38},{7,39},{8,40},{9,... | collective-permute-start | bytes 3735560 | tf_op jit(solution)/shard_map/ppermute | solution.py:49
  62.8 22.1 %collective-permute-start.14 = (bf16[2,2,304,512]{3,2,1,0:T(8,128)(2,1)}, bf16[2,2,304,512]{3,2,1,0:T(8,128)(2,1)S(1)}, u32[]{:S(2)}, u32[]{:S(2)}) collective-permute-start(bf16[2,2,304,512]{3,2,1,0:T(8,128)(2,1)} %get-tuple-element.74), channel_id=1, source_target_pairs={{0,32},{1,33},{2,34},{3,35},{4,36},{5,37},{6,38},{7,39},{8,40},{9,... | collective-permute-start | bytes 3735560 | tf_op jit(solution)/shard_map/ppermute | solution.py:49
  65.8 19.1 %copy-start.17 = (bf16[2,2,304,512]{3,2,1,0:T(8,128)(2,1)S(1)}, bf16[2,2,304,512]{3,2,1,0:T(8,128)(2,1)}, u32[]{:S(2)}) copy-start(bf16[2,2,304,512]{3,2,1,0:T(8,128)(2,1)} %get-tuple-element.73) | copy-start | bytes 3735556
  67.5 17.4 %collective-permute-start.16 = (bf16[2,304,512]{2,1,0:T(8,128)(2,1)S(1)}, bf16[2,304,512]{2,1,0:T(8,128)(2,1)S(1)}, u32[]{:S(2)}, u32[]{:S(2)}) collective-permute-start(bf16[2,304,512]{2,1,0:T(8,128)(2,1)S(1)} %get-tuple-element.97), channel_id=1, source_target_pairs={{0,192},{1,193},{2,194},{3,195},{4,196},{5,197},{6,198},{7,199},{8... | collective-permute-start | bytes 1867784 | tf_op jit(solution)/shard_map/ppermute | solution.py:49
  69.0 15.9 %collective-permute-start.17 = (bf16[2,304,512]{2,1,0:T(8,128)(2,1)S(1)}, bf16[2,304,512]{2,1,0:T(8,128)(2,1)S(1)}, u32[]{:S(2)}, u32[]{:S(2)}) collective-permute-start(bf16[2,304,512]{2,1,0:T(8,128)(2,1)S(1)} %get-tuple-element.96), channel_id=1, source_target_pairs={{0,64},{1,65},{2,66},{3,67},{4,68},{5,69},{6,70},{7,71},{8,72},{9,... | collective-permute-start | bytes 1867784 | tf_op jit(solution)/shard_map/ppermute | solution.py:49
  69.1 5.4 %collective-permute-start.18 = (bf16[128,512]{1,0:T(8,128)(2,1)S(1)}, bf16[128,512]{1,0:T(8,128)(2,1)S(1)}, u32[]{:S(2)}, u32[]{:S(2)}) collective-permute-start(bf16[128,512]{1,0:T(8,128)(2,1)S(1)} %get-tuple-element.101), channel_id=1, source_target_pairs={{0,30},{2,0},{4,2},{6,4},{8,6},{10,8},{12,10},{14,12},{16,14},{18,... | collective-permute-start | bytes 393224 | tf_op jit(solution)/shard_map/ppermute | solution.py:27
  71.6 7.1 %collective-permute-start.19 = (bf16[128,512]{1,0:T(8,128)(2,1)S(1)}, bf16[128,512]{1,0:T(8,128)(2,1)S(1)}, u32[]{:S(2)}, u32[]{:S(2)}) collective-permute-start(bf16[128,512]{1,0:T(8,128)(2,1)S(1)} %get-tuple-element.100), channel_id=1, source_target_pairs={{0,2},{2,4},{4,6},{6,8},{8,10},{10,12},{12,14},{14,16},{16,18},{18... | collective-permute-start | bytes 393224 | tf_op jit(solution)/shard_map/ppermute | solution.py:27
  84.9 0.8 copy-start.19
  84.9 1.0 copy-start.20
  84.9 1.4 %copy-start.18 = (bf16[2,2,304,512]{3,2,1,0:T(8,128)(2,1)}, bf16[2,2,304,512]{3,2,1,0:T(8,128)(2,1)S(1)}, u32[]{:S(2)}) copy-start(bf16[2,2,304,512]{3,2,1,0:T(8,128)(2,1)S(1)} %collective-permute-done.14) | copy-start | bytes 3735556
  86.3 8.6 %collective-permute-start.20 = (bf16[304,512]{1,0:T(8,128)(2,1)S(1)}, bf16[304,512]{1,0:T(8,128)(2,1)S(1)}, u32[]{:S(2)}, u32[]{:S(2)}) collective-permute-start(bf16[304,512]{1,0:T(8,128)(2,1)S(1)} %get-tuple-element.95), channel_id=1, source_target_pairs={{0,64},{1,65},{2,66},{3,67},{4,68},{5,69},{6,70},{7,71},{8,72},{9,... | collective-permute-start | bytes 933896 | tf_op jit(solution)/shard_map/ppermute | solution.py:49
  86.4 9.9 %collective-permute-start.21 = (bf16[304,512]{1,0:T(8,128)(2,1)S(1)}, bf16[304,512]{1,0:T(8,128)(2,1)}, u32[]{:S(2)}, u32[]{:S(2)}) collective-permute-start(bf16[304,512]{1,0:T(8,128)(2,1)S(1)} %get-tuple-element.94), channel_id=1, source_target_pairs={{0,192},{1,193},{2,194},{3,195},{4,196},{5,197},{6,198},{7,199},{8... | collective-permute-start | bytes 933896 | tf_op jit(solution)/shard_map/ppermute | solution.py:49
  98.3 6.7 %collective-permute-start.22 = (bf16[8,2,16,512]{3,2,1,0:T(8,128)(2,1)S(1)}, bf16[8,2,16,512]{3,2,1,0:T(8,128)(2,1)S(1)}, u32[]{:S(2)}, u32[]{:S(2)}) collective-permute-start(bf16[8,2,16,512]{3,2,1,0:T(8,128)(2,1)S(1)} %fusion.19), channel_id=1, source_target_pairs={{0,3},{1,2},{2,1},{3,0},{4,7},{5,6},{6,5},{7,4},{8,11},{9,10},{10,... | collective-permute-start | bytes 786440 | tf_op jit(solution)/shard_map/ppermute | solution.py:49
  105.1 26.1 %copy-start.8 = (s32[1,1,128]{2,1,0:T(1,128)S(1)}, s32[1,1,128]{2,1,0:T(1,128)}, u32[]{:S(2)}) copy-start(s32[1,1,128]{2,1,0:T(1,128)} %param.20) | copy-start | bytes 1540
  105.1 26.1 %copy-start.10 = (s32[1,1,8]{2,1,0:T(1,128)S(1)}, s32[1,1,8]{2,1,0:T(1,128)}, u32[]{:S(2)}) copy-start(s32[1,1,8]{2,1,0:T(1,128)} %param.21) | copy-start | bytes 100
  105.2 6.4 %collective-permute-start.23 = (bf16[8,24,512]{2,1,0:T(8,128)(2,1)S(1)}, bf16[8,24,512]{2,1,0:T(8,128)(2,1)S(1)}, u32[]{:S(2)}, u32[]{:S(2)}) collective-permute-start(bf16[8,24,512]{2,1,0:T(8,128)(2,1)S(1)} %fusion.23), channel_id=1, source_target_pairs={{0,2},{1,3},{2,0},{3,1},{4,6},{5,7},{6,4},{7,5},{8,10},{9,11},{10,... | collective-permute-start | bytes 589832 | tf_op jit(solution)/shard_map/ppermute | solution.py:49
  107.2 4.4 %collective-permute-start.24 = (bf16[128,512]{1,0:T(8,128)(2,1)S(1)}, bf16[128,512]{1,0:T(8,128)(2,1)S(1)}, u32[]{:S(2)}, u32[]{:S(2)}) collective-permute-start(bf16[128,512]{1,0:T(8,128)(2,1)S(1)} %get-tuple-element.99), channel_id=1, source_target_pairs={{32,0},{64,32},{96,64},{128,96},{160,128},{192,160},{224,192},{33,... | collective-permute-start | bytes 393224 | tf_op jit(solution)/shard_map/ppermute | solution.py:21
  108.5 4.0 %collective-permute-start.25 = (bf16[128,512]{1,0:T(8,128)(2,1)S(1)}, bf16[128,512]{1,0:T(8,128)(2,1)S(1)}, u32[]{:S(2)}, u32[]{:S(2)}) collective-permute-start(bf16[128,512]{1,0:T(8,128)(2,1)S(1)} %get-tuple-element.98), channel_id=1, source_target_pairs={{0,32},{32,64},{64,96},{96,128},{128,160},{160,192},{192,224},{1,3... | collective-permute-start | bytes 393224 | tf_op jit(solution)/shard_map/ppermute | solution.py:21
  112.5 5.7 %collective-permute-start.26 = (bf16[2,2,24,512]{3,2,1,0:T(8,128)(2,1)S(1)}, bf16[2,2,24,512]{3,2,1,0:T(8,128)(2,1)S(1)}, u32[]{:S(2)}, u32[]{:S(2)}) collective-permute-start(bf16[2,2,24,512]{3,2,1,0:T(8,128)(2,1)S(1)} %dynamic-slice_bitcast_fusion), channel_id=1, source_target_pairs={{0,4},{1,5},{2,6},{3,7},{4,0},{5,1},{6,2},{7,3},{8,12},{9,13},{10,... | collective-permute-start | bytes 294920 | tf_op jit(solution)/shard_map/ppermute | solution.py:49
  118.3 5.1 %collective-permute-start.27 = (bf16[2,24,512]{2,1,0:T(8,128)(2,1)S(1)}, bf16[2,24,512]{2,1,0:T(8,128)(2,1)S(1)}, u32[]{:S(2)}, u32[]{:S(2)}) collective-permute-start(bf16[2,24,512]{2,1,0:T(8,128)(2,1)S(1)} %dynamic-slice_bitcast_fusion.1), channel_id=1, source_target_pairs={{0,8},{1,9},{2,10},{3,11},{4,12},{5,13},{6,14},{7,15},{8,0},{9,1},... | collective-permute-start | bytes 147464 | tf_op jit(solution)/shard_map/ppermute | solution.py:49
  123.4 7.8 %collective-permute-start.28 = (bf16[24,512]{1,0:T(8,128)(2,1)S(1)}, bf16[24,512]{1,0:T(8,128)(2,1)S(1)}, u32[]{:S(2)}, u32[]{:S(2)}) collective-permute-start(bf16[24,512]{1,0:T(8,128)(2,1)S(1)} %get-tuple-element.104), channel_id=1, source_target_pairs={{0,16},{1,17},{2,18},{3,19},{4,20},{5,21},{6,22},{7,23},{8,24},{9,... | collective-permute-start | bytes 73736 | tf_op jit(solution)/shard_map/ppermute | solution.py:49
  (2 other events, 1.3 us)

commit v2 on v1

--- a/solution.py
+++ b/solution.py
@@ -13,18 +13,6 @@
 BF16 = jnp.bfloat16
 WIDTH = 512
 UNIT = 304
-
-
-def shifted(block, axis, distance):
-    devices = range(lax.axis_size(axis))
-    route = [(i - distance, i) for i in devices if i - distance in devices]
-    return lax.ppermute(block, axis, route)
-
-
-def from_behind(value, axis, steps):
-    count = lax.axis_size(axis)
-    pairs = [(source, (source + steps) % count) for source in range(count)]
-    return lax.ppermute(value, axis, pairs)
 
 
 def partner_of(index, kind, amount):
@@ -41,12 +29,18 @@
     elif kind == "y":
         y_lo ^= amount & 1
         y_hi ^= amount >> 1
+    elif kind == "next band":
+        x, core = x + (2 * core - 1), 1 - core
+        if not 0 <= x < 4:
+            return None
+    elif kind == "next sector":
+        z, y_lo = (z + 2 * y_lo - 1) & 7, 1 - y_lo
     return ((x * 2 + core) * 8 + z) * 4 + y_lo * 2 + y_hi
 
 
 def exchange(value, kind, amount=1):
     pairs = [(i, partner_of(i, kind, amount)) for i in range(256)]
-    return lax.ppermute(value, AXES, pairs)
+    return lax.ppermute(value, AXES, [pair for pair in pairs if pair[1] is not None])
 
 
 def position():
@@ -74,6 +68,13 @@
     return dcore * 512 + half * 256 + xslot * 64 + (zslot & 3) * 16 + dy * 8 + within
 
 
+def rim_slot(row):
+    _, core, _, y_lo, _ = position()
+    axis, upper = row >> 8, row >> 7 & 1
+    block = upper ^ 1 ^ jnp.where(axis == 0, core, y_lo)
+    return axis * 256 + block * 128 + (row & 127)
+
+
 def plus(*values):
     total = values[0].astype(F32)
     for value in values[1:]:
@@ -85,18 +86,23 @@
     return lax.dynamic_index_in_dim(array, which, axis, keepdims=False)
 
 
-def reduce_all(keep_far, send_far, keep_near, send_near, rim_grad):
+def reduce_all(rim_grads, keep_far, send_far, keep_near, send_near):
     _, _, z, y_lo, y_hi = position()
     got_far = exchange(send_far, "core")
+    to_core, to_band, to_y, to_sector = rim_grads
+    back_core = exchange(to_core, "core")
     got_near = exchange(send_near, "core")
     got_a = exchange(plus(keep_far[0], got_far[0]), "x", 3)
     got_b = exchange(plus(keep_far[1], got_far[1]), "x", 1)
-    back_lon = [from_behind(rim_grad[128 * k : 128 * k + 128], "lon", step) for k, step in ((2, -1), (3, 1))]
-    got_a, got_b, *back_lon = lax.optimization_barrier((got_a, got_b, *back_lon))
-    new_a = exchange(plus(keep_near[0, 1], got_near[0, 1], got_a[1]), "x", 1)
-    new_b = exchange(plus(keep_near[1, 1], got_near[1, 1], got_b[1]), "x", 3)
-    new_a, new_b, rim_grad = lax.optimization_barrier((new_a, new_b, rim_grad))
-    back_lat = [shifted(rim_grad[128 * k : 128 * k + 128], "lat", step) for k, step in ((0, -1), (1, 1))]
+    back_band = exchange(to_band, "next band")
+    back_sector = exchange(to_sector, "next sector")
+    got_a, got_b, to_y, back_core, back_band, back_sector = lax.optimization_barrier(
+        (got_a, got_b, to_y, back_core, back_band, back_sector)
+    )
+    next_a = plus(keep_near[0, 1], got_near[0, 1], got_a[1])
+    next_b = plus(keep_near[1, 1], got_near[1, 1], got_b[1])
+    next_a, next_b = lax.optimization_barrier((next_a, next_b))
+    new_a, new_b = exchange(next_a, "x", 1), exchange(next_b, "x", 3)
     a = plus(keep_near[0, 0], got_near[0, 0], got_a[0], new_a)
     b = plus(keep_near[1, 0], got_near[1, 0], got_b[0], new_b)
     weights = jnp.concatenate([a[:224], b[:224]], axis=0).reshape(8, 4, 14, WIDTH)
@@ -106,15 +112,17 @@
     got = exchange(pick(units, 1 - y_hi, 2), "y", 3)
     units = plus(pick(units, y_hi, 2), got)
     units = jnp.concatenate([units, coarse], axis=2)
+    units, to_y = lax.optimization_barrier((units, to_y))
     got = exchange(pick(units, 1 - y_lo, 1), "y", 1)
+    back_y = exchange(to_y, "y")
     units = plus(pick(units, y_lo, 1), got).reshape(2, 2, 2, 24, WIDTH)
-    units, *back_lat = lax.optimization_barrier((units, *back_lat))
     got = exchange(pick(units, 1 - (z & 1), 2), "z", 1)
     units = plus(pick(units, z & 1, 2), got)
     got = exchange(pick(units, 1 - (z >> 1 & 1), 1), "z", 2)
     units = plus(pick(units, z >> 1 & 1, 1), got)
+    units, back_y = lax.optimization_barrier((units, back_y))
     got = exchange(pick(units, 1 - (z >> 2)), "z", 4)
-    return pick(units, z >> 2), got, back_lat + back_lon
+    return pick(units, z >> 2), got, (back_core, back_band, back_y, back_sector)
 
 
 def dot(a, b, ca=1, cb=0):
@@ -153,10 +161,14 @@
     return gate * (1.0 + pre * (1.0 - gate))
 
 
-def outgoing_kernel(rim_ref, coarse_ref, nodes_ref, rows_ref, coarse_rows_ref):
+def outgoing_kernel(rim_ref, coarse_ref, nodes_hbm, rows_ref, coarse_rows_ref, nodes_ref, sems):
+    wait = fetch(((nodes_hbm, nodes_ref),), sems)
+    rims = one_hot(down(rim_ref[...], 128), 0, 256)
+    coarse = one_hot_t(coarse_ref[...], 0, 256)
+    wait(0)
     nodes = nodes_ref[...]
-    rows_ref[...] = dot(one_hot(down(rim_ref[...], 128), 0, 256), nodes).astype(BF16)
-    coarse_rows_ref[...] = dot(one_hot_t(coarse_ref[...], 0, 256), nodes, 0, 0).astype(BF16)
+    coarse_rows_ref[...] = dot(coarse, nodes, 0, 0).astype(BF16)
+    rows_ref[...] = dot(rims, nodes).astype(BF16)
 
 
 def fetch(pairs, sems):
@@ -166,67 +178,19 @@
     return lambda n: copies[n].wait()
 
 
-def near_kernel(
-    index_ref,
-    nodes_hbm,
-    edges_hbm,
-    w_ein_hbm,
-    w_nin_hbm,
-    pre_ref,
-    node_pre_ref,
-    recv_rows_ref,
-    own_rows_ref,
-    nodes_ref,
-    edges_ref,
-    w_ein_ref,
-    w_nin_ref,
-    sems,
-):
-    wait = fetch(
-        (
-            (nodes_hbm, nodes_ref),
-            (w_ein_hbm, w_ein_ref),
-            (edges_hbm, edges_ref),
-            (w_nin_hbm.at[0:512], w_nin_ref),
-        ),
-        sems,
-    )
-    slots = one_hot(down(index_ref[0:1], 384), 0, 256)
-    receivers = one_hot(down(index_ref[2:3], 384), 0, 256)
-    wait(0)
-    nodes = nodes_ref[...]
-    recv_rows = dot(receivers, nodes).astype(BF16)
-    own_rows = dot(slots, nodes).astype(BF16)
-    recv_rows_ref[...] = recv_rows
-    own_rows_ref[...] = own_rows
-    wait(1)
-    wait(2)
-    pre_ref[...] = (
-        dot(own_rows, w_ein_ref[0:512])
-        + dot(recv_rows, w_ein_ref[512:1024])
-        + dot(edges_ref[...], w_ein_ref[1024:1536])
-    )
-    wait(3)
-    node_pre_ref[...] = dot(nodes, w_nin_ref[...])
-
-
 def layer_kernel(
     place_ref,
     index_ref,
-    pre_ref,
-    node_pre_ref,
-    recv_rows_ref,
-    own_rows_ref,
     edges_hbm,
     nodes_hbm,
-    lower_ref,
-    upper_ref,
-    west_ref,
-    east_ref,
-    near_top_ref,
-    near_low_ref,
-    far_top_ref,
-    far_low_ref,
+    rim_core_hbm,
+    rim_band_hbm,
+    rim_y_hbm,
+    rim_sector_hbm,
+    near_top_hbm,
+    near_low_hbm,
+    far_top_hbm,
+    far_low_hbm,
     w_ein_hbm,
     w_eout_hbm,
     w_nin_hbm,
@@ -239,11 +203,14 @@
     new_edges_hbm,
     edge_grad_hbm,
     own_grad_hbm,
-    rim_grad_ref,
-    keep_far_ref,
-    send_far_ref,
-    keep_near_ref,
-    send_near_ref,
+    to_core_ref,
+    to_band_ref,
+    to_y_ref,
+    to_sector_ref,
+    keep_far_hbm,
+    send_far_hbm,
+    keep_near_hbm,
+    send_near_hbm,
     big_ref,
     coarse_ref,
     unit_ref,
@@ -259,43 +226,51 @@
     new_edges_ref,
     edge_grad_ref,
     own_grad_ref,
+    far_rows_ref,
+    gains_ref,
+    move_sems,
+    coarse_sems,
     sems,
     out_sems,
 ):
+    pieces = (rim_core_hbm, rim_band_hbm, rim_y_hbm, rim_sector_hbm, near_top_hbm, near_low_hbm, far_top_hbm, far_low_hbm)
+    starts = (0, 128, 256, 384, 512, 768, 1024, 1280, 1536)
     wait = fetch(
         (
+            *[(piece, far_rows_ref.at[lo:hi]) for piece, lo, hi in zip(pieces, starts, starts[1:])],
+            (nodes_hbm, nodes_ref),
             (w_ein_hbm, w_ein_ref),
+            (edges_hbm, edges_ref),
             (w_eout_hbm, w_eout_ref),
-            (edges_hbm, edges_ref),
             (w_nin_hbm, w_nin_ref),
             (w_nout_hbm, w_nout_ref),
-            (nodes_hbm, nodes_ref),
             (node_cot_hbm, node_cot_ref),
             (edge_cot_hbm, edge_cot_ref),
         ),
         sems,
     )
     slots = down(index_ref[0:1], 384)
-    lower_upper = jnp.concatenate([lower_ref[...], upper_ref[...]], axis=0)
-    west_east = jnp.concatenate([west_ref[...], east_ref[...]], axis=0)
-    far = (
-        dot(one_hot(slots, 256, 256), lower_upper)
-        + dot(one_hot(slots, 512, 256), west_east)
-        + dot(one_hot(slots, 768, 256), near_top_ref[...])
-        + dot(one_hot(slots, 1024, 256), near_low_ref[...])
-        + dot(one_hot(slots, 1280, 256), far_top_ref[...])
-        + dot(one_hot(slots, 1536, 256), far_low_ref[...])
-    ).astype(BF16)
-    send_rows = (far.astype(F32) + own_rows_ref[...].astype(F32)).astype(BF16)
-    wait(0)
-    pre = pre_ref[...] + dot(far, w_ein_ref[0:512])
+    receivers = one_hot(down(index_ref[2:3], 384), 0, 256)
+    near = one_hot(slots, 0, 256)
+    far = one_hot(slots, 256, 1536)
+    for n in range(9):
+        wait(n)
+    nodes = nodes_ref[...]
+    send_rows = (dot(far, far_rows_ref[...]) + dot(near, nodes)).astype(BF16)
+    recv_rows = dot(receivers, nodes).astype(BF16)
+    wait(9)
+    wait(10)
+    pre = (
+        dot(send_rows, w_ein_ref[0:512])
+        + dot(recv_rows, w_ein_ref[512:1024])
+        + dot(edges_ref[...], w_ein_ref[1024:1536])
+    )
     hidden = (pre * jax.nn.sigmoid(pre)).astype(BF16)
     gain_e = gain_e_ref[...]
-    wait(1)
+    wait(11)
     unit, scale = normed(dot(hidden, w_eout_ref[...]))
     unit_ref[...] = unit
     message = unit * gain_e
-    wait(2)
     new_edges_ref[...] = (edges_ref[...].astype(F32) + message).astype(BF16)
     new_edges_out = pltpu.make_async_copy(new_edges_ref, new_edges_hbm, out_sems.at[0])
     new_edges_out.start()
@@ -303,11 +278,10 @@
     coarse_part = message.astype(BF16)
     fine_part = (message - coarse_part.astype(F32)).astype(BF16)
     pooled = (dot(into, coarse_part) + dot(into, fine_part)).astype(BF16)
-    for n in (3, 4, 5, 6, 7):
+    for n in (12, 13, 14, 15):
         wait(n)
-    nodes = nodes_ref[...]
     gain_n = gain_n_ref[...]
-    node_pre = node_pre_ref[...] + dot(pooled, w_nin_ref[512:1024])
+    node_pre = dot(nodes, w_nin_ref[0:512]) + dot(pooled, w_nin_ref[512:1024])
     node_hidden = (node_pre * jax.nn.sigmoid(node_pre)).astype(BF16)
     node_unit, node_scale = normed(dot(node_hidden, w_nout_ref[...]))
     new_nodes_ref[...] = (nodes.astype(F32) + node_unit * gain_n).astype(BF16)
@@ -331,17 +305,39 @@
     big_ref[1536:2048] = dot(hidden, back, 0, 0).astype(BF16)
     back = dot(back, w_eout_ref[...], 1, 1).astype(BF16).astype(F32)
     back = (back * silu_slope(pre)).astype(BF16)
+    big_ref[0:512] = dot(send_rows, back, 0, 0).astype(BF16)
+    big_ref[512:1024] = dot(recv_rows, back, 0, 0).astype(BF16)
+    big_ref[1024:1536] = dot(edges_ref[...], back, 0, 0).astype(BF16)
+    row = lax.broadcasted_iota(jnp.int32, (16, WIDTH), 0)
+    gains = jnp.where(row == 0, gain_grad_e, jnp.where(row == 1, gain_grad_n, 0.0))
+    gains_ref[...] = gains.astype(BF16)
+    x, core = place_ref[0], place_ref[1]
+    moves, coarse_moves = [], []
+    for half, offsets in ((0, (0, 1, 3, 2)), (1, (0, 3, 1, 2))):
+        for at, offset in enumerate(offsets):
+            sides = (keep_far_hbm, send_far_hbm) if at >= 2 else (keep_near_hbm, send_near_hbm)
+            for ref, other in zip(sides, (core, 1 - core)):
+                block = (x ^ offset) * 2 + other
+                unit = ref.at[half, at % 2]
+                rows = pl.ds(pl.multiple_of(block * 448 + half * 224, 32), 224)
+                moves.append((big_ref.at[rows], unit.at[0:224]))
+                moves.append((gains_ref, unit.at[288:304]))
+                rows = pl.ds(pl.multiple_of(block * 128 + half * 64, 64), 64)
+                coarse_moves.append((coarse_ref.at[rows], unit.at[224:288]))
+    weights_left = fetch(moves, move_sems)
     send_grad = dot(back, w_ein_ref[0:512], 1, 1).astype(BF16)
     recv_grad = dot(back, w_ein_ref[512:1024], 1, 1).astype(BF16)
-    big_ref[0:512] = dot(send_rows, back, 0, 0).astype(BF16)
-    big_ref[512:1024] = dot(recv_rows_ref[...], back, 0, 0).astype(BF16)
-    big_ref[1024:1536] = dot(edges_ref[...], back, 0, 0).astype(BF16)
+    senders = index_ref[1:2]
+    coarse_ref[...] = dot(one_hot_t(senders, 768, 1024), send_grad).astype(BF16)
+    coarse_left = fetch(coarse_moves, coarse_sems)
+    rim_grad = dot(one_hot_t(index_ref[0:1], 256, 512), send_grad).astype(BF16)
+    for at, ref in enumerate((to_core_ref, to_band_ref, to_y_ref, to_sector_ref)):
+        ref[...] = rim_grad[128 * at : 128 * at + 128]
     edge_grad_ref[...] = (
         edge_cot + dot(back, w_ein_ref[1024:1536], 1, 1).astype(BF16).astype(F32)
     ).astype(BF16)
     edge_grad_out = pltpu.make_async_copy(edge_grad_ref, edge_grad_hbm, out_sems.at[2])
     edge_grad_out.start()
-    senders = index_ref[1:2]
     own_grad_ref[...] = (
         own_grad
         + dot(one_hot_t(index_ref[2:3], 0, 256), recv_grad)
@@ -349,21 +345,10 @@
     )
     own_grad_out = pltpu.make_async_copy(own_grad_ref, own_grad_hbm, out_sems.at[3])
     own_grad_out.start()
-    rim_grad_ref[...] = dot(one_hot_t(senders, 256, 512), send_grad).astype(BF16)
-    coarse_ref[...] = dot(one_hot_t(senders, 768, 1024), send_grad).astype(BF16)
-    row = lax.broadcasted_iota(jnp.int32, (16, WIDTH), 0)
-    gains = jnp.where(row == 0, gain_grad_e, jnp.where(row == 1, gain_grad_n, 0.0)).astype(BF16)
-    x, core = place_ref[0], place_ref[1]
-    for half, offsets in ((0, (0, 1, 3, 2)), (1, (0, 3, 1, 2))):
-        for at, offset in enumerate(offsets):
-            sides = (keep_far_ref, send_far_ref) if at >= 2 else (keep_near_ref, send_near_ref)
-            for ref, other in zip(sides, (core, 1 - core)):
-                block = (x ^ offset) * 2 + other
-                rows = pl.ds(pl.multiple_of(block * 448 + half * 224, 32), 224)
-                ref[half, at % 2, 0:224] = big_ref[rows]
-                rows = pl.ds(pl.multiple_of(block * 128 + half * 64, 64), 64)
-                ref[half, at % 2, 224:288] = coarse_ref[rows]
-                ref[half, at % 2, 288:304] = gains
+    for n in range(len(moves)):
+        weights_left(n)
+    for n in range(len(coarse_moves)):
+        coarse_left(n)
     for copy in (new_edges_out, new_nodes_out, edge_grad_out, own_grad_out):
         copy.wait()
 
@@ -389,7 +374,7 @@
     out_ref[...] = total.astype(BF16)
 
 
-def call(kernel, out, *operands, scratch=(), small=(), there=(), out_there=(), flops=0, limit=48):
+def call(kernel, out, *operands, scratch=(), small=(), there=(), out_there=(), flops=0, limit=50):
     def spec(at, away):
         return pl.BlockSpec(memory_space=pltpu.SMEM if at in small else pltpu.HBM if at in away else pltpu.VMEM)
 
@@ -433,52 +418,36 @@
         rim_list,
         coarse_ids,
         nodes,
+        scratch=[pltpu.VMEM((256, WIDTH), BF16), pltpu.SemaphoreType.DMA((1,))],
+        there=(2,),
         flops=2 * 136 * 256 * 512,
         limit=16,
     )
-    rims = [shifted(outgoing, "lat", step) for step in (1, -1)]
-    slot = jnp.where(send >= 768, 768 + coarse_slot(send - 768), send)
+    far = jnp.where(send >= 768, 768 + coarse_slot(send - 768), 256 + rim_slot(send - 256))
+    slot = jnp.where(send < 256, send, far)
     live_recv = jnp.where(edge_live[0] != 0, recv, -1)
     index = jnp.concatenate([slot, send, recv, live_recv, slot, slot, slot, slot], axis=0)
-    pre, node_pre, recv_rows, own_rows = call(
-        near_kernel,
-        [((384, WIDTH), F32), ((256, WIDTH), F32), ((384, WIDTH), BF16), ((384, WIDTH), BF16)],
-        index,
-        nodes,
-        edges,
-        edge_in_w,
-        node_in_w,
-        scratch=[
-            pltpu.VMEM((256, WIDTH), BF16),
-            pltpu.VMEM((384, WIDTH), BF16),
-            pltpu.VMEM((1536, WIDTH), BF16),
-            pltpu.VMEM((512, WIDTH), BF16),
-            pltpu.SemaphoreType.DMA((4,)),
-        ],
-        there=(1, 2, 3, 4),
-        flops=2 * 384 * 2048 * 512,
-        limit=24,
-    )
-    rows = doubled(coarse_own, ("y", 1), ("ring", 1), ("ring", -1))
-    rows, *rims = lax.optimization_barrier((rows, *rims))
+    rows = doubled(coarse_own, ("y", 1))
+    rim_y, rim_sector = exchange(outgoing, "y"), exchange(outgoing, "next sector")
+    rim_band = exchange(outgoing, "next band")
+    rows = doubled(rows, ("ring", 1))
+    rows, outgoing, rim_y, rim_band, rim_sector = lax.optimization_barrier((rows, outgoing, rim_y, rim_band, rim_sector))
+    rows = doubled(rows, ("ring", -1))
     rows = doubled(rows, ("ring", 3))
-    rows, outgoing, pre, node_pre, recv_rows, own_rows = lax.optimization_barrier(
-        (rows, outgoing, pre, node_pre, recv_rows, own_rows)
-    )
     top, low = doubled(rows[:64], ("x", 1)), doubled(rows[64:], ("x", 3))
-    rims += [from_behind(outgoing, "lon", step) for step in (1, -1)]
-    top, low, *rims = lax.optimization_barrier((top, low, *rims))
+    top, low, outgoing = lax.optimization_barrier((top, low, outgoing))
     gathered = [doubled(top, ("x", 3)), doubled(low, ("x", 1))]
     gathered += [exchange(rows, "core") for rows in gathered]
+    rims = exchange(outgoing, "core"), rim_band, rim_y, rim_sector
     place = jnp.stack([x, core]).astype(jnp.int32)
-    new_nodes, new_edges, edge_grad, own_grad, rim_grad, *units = call(
+    new_nodes, new_edges, edge_grad, own_grad, *sums = call(
         layer_kernel,
         [
             ((256, WIDTH), BF16),
             ((384, WIDTH), BF16),
             ((384, WIDTH), BF16),
             ((256, WIDTH), F32),
-            ((512, WIDTH), BF16),
+            *[((128, WIDTH), BF16)] * 4,
             ((2, 2, UNIT, WIDTH), BF16),
             ((2, 2, UNIT, WIDTH), BF16),
             ((2, 2, UNIT, WIDTH), BF16),
@@ -486,10 +455,6 @@
         ],
         place,
         index,
-        pre,
-        node_pre,
-        recv_rows,
-        own_rows,
         edges,
         nodes,
         *rims,
@@ -518,15 +483,19 @@
             pltpu.VMEM((384, WIDTH), BF16),
             pltpu.VMEM((384, WIDTH), BF16),
             pltpu.VMEM((256, WIDTH), F32),
-            pltpu.SemaphoreType.DMA((8,)),
+            pltpu.VMEM((1536, WIDTH), BF16),
+            pltpu.VMEM((16, WIDTH), BF16),
+            pltpu.SemaphoreType.DMA((32,)),
+            pltpu.SemaphoreType.DMA((16,)),
+            pltpu.SemaphoreType.DMA((16,)),
             pltpu.SemaphoreType.DMA((4,)),
         ],
         small=(0,),
-        there=(6, 7, 16, 17, 18, 19, 22, 23),
-        out_there=(0, 1, 2, 3),
+        there=(2, 3, 4, 5, 6, 7, 8, 9, 10, 11, 12, 13, 14, 15, 18, 19),
+        out_there=(0, 1, 2, 3, 8, 9, 10, 11),
         flops=2 * 384 * 512 * 10000,
     )
-    kept, got, back = reduce_all(*units, rim_grad)
+    kept, got, back = reduce_all(sums[:4], *sums[4:])
     devices = lax.axis_size("lat") * lax.axis_size("lon") * lax.axis_size("dp")
     node_grad, weight_share, gain_grad = call(
         functools.partial(finish_kernel, 1.0 / math.sqrt(384 * devices)),

time: 135 us -> 133 us (0.985)
  waiting for transfers between devices: 54.6 us -> 58.8 us
  starting transfers between devices: 46.6 us -> 43.7 us
  local copies, waits for them, and re-layouts: 9.68 us -> 7.12 us
    ppermute x29, waiting for transfers between devices: 54.6 us -> 58.8 us  [exchange(): lax.ppermute(value, AXES, [pair for pair in pairs if pair[1] is not None])]
    unnamed x44 -> x41, local copies, waits for them, and re-layouts: 8.01 us -> 3.8 us
    ppermute x29, starting transfers between devices: 46.6 us -> 43.7 us  [exchange(): lax.ppermute(value, AXES, [pair for pair in pairs if pair[1] is not None])]
    pallas_call x4 -> x3, Pallas kernels: 16.4 us -> 15.7 us  [call(): pl.pallas_call(kernel, out_shape=[jax.ShapeDtypeStruct(*leaf) for leaf in...]
  transfers between devices with their start and end apart: 29 -> 29, of which waited for: 17 -> 20; matrix products, arithmetic and copies ran while one was open for 3% -> 3% of each run, Pallas kernels for 2% -> 0%
where the time goes in v2:
time: 133 us; the launch traced here: 131 us
  waiting for transfers between devices  58.8 us (44%)
  starting transfers between devices  43.7 us (33%)
  Pallas kernels  15.7 us (12%)
  local copies, waits for them, and re-layouts  7.12 us (5%)
  other arithmetic  4.95 us (4%)
    ppermute x29, waiting for transfers between devices, exchange(): lax.ppermute(value, AXES, [pair for pair in pairs if pair[1] is not None])  58.8 us
    ppermute x29, starting transfers between devices, exchange(): lax.ppermute(value, AXES, [pair for pair in pairs if pair[1] is not None])  43.7 us
    pallas_call x3, Pallas kernels, call(): pl.pallas_call(kernel, out_shape=[jax.ShapeDtypeStruct(*leaf) for leaf in...  15.7 us
    convert_element_type x7, other arithmetic, plus(): return total.astype(BF16)  4.66 us
    unnamed x41, local copies, waits for them, and re-layouts  3.8 us
  transfers between devices with their start and end apart: 29, of which 20 were waited for; matrix products, arithmetic and copies ran while one was open for 3% of the time, Pallas kernels for 0%

profile of v2, /device:TPU:16, one launch (start us, length us, event | category | flops | bytes accessed | tf_op | source)
XLA Modules:
  0.0 131.3 jit_solution(5378882571717783254)
XLA Ops:
  0.7 1.0 copy-done
  1.6 0.7 copy-done.2
  3.4 1.4 %collective-permute-start = (bf16[8,512]{1,0:T(8,128)(2,1)S(1)}, bf16[8,512]{1,0:T(8,128)(2,1)S(1)}, u32[]{:S(2)}, u32[]{:S(2)}) collective-permute-start(bf16[8,512]{1,0:T(8,128)(2,1)S(1)} %get-tuple-element.43), channel_id=1, source_target_pairs={{0,2},{1,3},{2,0},{3,1},{4,6},{5,7},{6,4},{7,5},{8,10},{9,11},{10,... | collective-permute-start | bytes 24584 | tf_op jit(solution)/shard_map/ppermute | solution.py:43
  4.7 0.7 collective-permute-start.2
  5.5 0.7 collective-permute-start.3
  6.1 6.7 %collective-permute-start.4 = (bf16[128,512]{1,0:T(8,128)(2,1)S(1)}, bf16[128,512]{1,0:T(8,128)(2,1)S(1)}, u32[]{:S(2)}, u32[]{:S(2)}) collective-permute-start(bf16[128,512]{1,0:T(8,128)(2,1)S(1)} %get-tuple-element.47), channel_id=1, source_target_pairs={{0,30},{1,31},{2,4},{3,5},{4,2},{5,3},{6,8},{7,9},{8,6},{9,7},{10,... | collective-permute-start | bytes 393224 | tf_op jit(solution)/shard_map/ppermute | solution.py:43
  12.8 3.7 %collective-permute-done.1 = bf16[16,512]{1,0:T(8,128)(2,1)S(1)} collective-permute-done((bf16[16,512]{1,0:T(8,128)(2,1)S(1)}, bf16[16,512]{1,0:T(8,128)(2,1)S(1)}, u32[]{:S(2)}, u32[]{:S(2)}) %collective-permute-start.1) | collective-permute-done | bytes 16416 | tf_op jit(solution)/shard_map/ppermute | solution.py:43
  16.6 1.4 %collective-permute-start.5 = (bf16[32,512]{1,0:T(8,128)(2,1)S(1)}, bf16[32,512]{1,0:T(8,128)(2,1)S(1)}, u32[]{:S(2)}, u32[]{:S(2)}) collective-permute-start(bf16[32,512]{1,0:T(8,128)(2,1)S(1)} %pad_maximum_fusion.5), channel_id=1, source_target_pairs={{0,28},{1,29},{2,30},{3,31},{4,8},{5,9},{6,10},{7,11},{8,4},{9,5},... | collective-permute-start | bytes 98312 | tf_op jit(solution)/shard_map/ppermute | solution.py:43
  17.9 3.8 %collective-permute-done.5 = bf16[32,512]{1,0:T(8,128)(2,1)S(1)} collective-permute-done((bf16[32,512]{1,0:T(8,128)(2,1)S(1)}, bf16[32,512]{1,0:T(8,128)(2,1)S(1)}, u32[]{:S(2)}, u32[]{:S(2)}) %collective-permute-start.5) | collective-permute-done | bytes 32800 | tf_op jit(solution)/shard_map/ppermute | solution.py:43
  21.8 1.2 collective-permute-start.7
  22.9 3.6 %collective-permute-start.6 = (bf16[64,512]{1,0:T(8,128)(2,1)S(1)}, bf16[64,512]{1,0:T(8,128)(2,1)S(1)}, u32[]{:S(2)}, u32[]{:S(2)}) collective-permute-start(bf16[64,512]{1,0:T(8,128)(2,1)S(1)} %constant_dynamic-update-slice_fusion), channel_id=1, source_target_pairs={{0,64},{1,65},{2,66},{3,67},{4,68},{5,69},{6,70},{7,71},{8,72},{9,... | collective-permute-start | bytes 196616 | tf_op jit(solution)/shard_map/ppermute | solution.py:43
  26.6 2.1 %collective-permute-done.7 = bf16[64,512]{1,0:T(8,128)(2,1)S(1)} collective-permute-done((bf16[64,512]{1,0:T(8,128)(2,1)S(1)}, bf16[64,512]{1,0:T(8,128)(2,1)S(1)}, u32[]{:S(2)}, u32[]{:S(2)}) %collective-permute-start.7) | collective-permute-done | bytes 65568 | tf_op jit(solution)/shard_map/ppermute | solution.py:43
  28.7 3.2 %collective-permute-start.8 = (bf16[64,512]{1,0:T(8,128)(2,1)S(1)}, bf16[64,512]{1,0:T(8,128)(2,1)S(1)}, u32[]{:S(2)}, u32[]{:S(2)}) collective-permute-start(bf16[64,512]{1,0:T(8,128)(2,1)S(1)} %collective-permute-done.7), channel_id=1, source_target_pairs={{0,192},{1,193},{2,194},{3,195},{4,196},{5,197},{6,198},{7,199},{8... | collective-permute-start | bytes 196616 | tf_op jit(solution)/shard_map/ppermute | solution.py:43
  31.9 2.2 %collective-permute-done.8 = bf16[64,512]{1,0:T(8,128)(2,1)S(1)} collective-permute-done((bf16[64,512]{1,0:T(8,128)(2,1)S(1)}, bf16[64,512]{1,0:T(8,128)(2,1)S(1)}, u32[]{:S(2)}, u32[]{:S(2)}) %collective-permute-start.8) | collective-permute-done | bytes 65568 | tf_op jit(solution)/shard_map/ppermute | solution.py:43
  34.2 0.8 collective-permute-start.11
  35.0 2.7 %collective-permute-start.10 = (bf16[128,512]{1,0:T(8,128)(2,1)S(1)}, bf16[128,512]{1,0:T(8,128)(2,1)S(1)}, u32[]{:S(2)}, u32[]{:S(2)}) collective-permute-start(bf16[128,512]{1,0:T(8,128)(2,1)S(1)} %pad_maximum_fusion.2), channel_id=1, source_target_pairs={{0,192},{1,193},{2,194},{3,195},{4,196},{5,197},{6,198},{7,199},{8... | collective-permute-start | bytes 393224 | tf_op jit(solution)/shard_map/ppermute | solution.py:43
  37.7 1.5 %collective-permute-done.11 = bf16[128,512]{1,0:T(8,128)(2,1)S(1)} collective-permute-done((bf16[128,512]{1,0:T(8,128)(2,1)S(1)}, bf16[128,512]{1,0:T(8,128)(2,1)S(1)}, u32[]{:S(2)}, u32[]{:S(2)}) %collective-permute-start.11) | collective-permute-done | bytes 131104 | tf_op jit(solution)/shard_map/ppermute | solution.py:43
  39.4 1.9 %collective-permute-done.10 = bf16[128,512]{1,0:T(8,128)(2,1)S(1)} collective-permute-done((bf16[128,512]{1,0:T(8,128)(2,1)S(1)}, bf16[128,512]{1,0:T(8,128)(2,1)S(1)}, u32[]{:S(2)}, u32[]{:S(2)}) %collective-permute-start.10) | collective-permute-done | bytes 131104 | tf_op jit(solution)/shard_map/ppermute | solution.py:43
  41.6 0.7 concatenate.41.index_ref
  43.1 0.7 copy-done.10
  43.8 13.8 %shard_map.191 = (bf16[256,512]{1,0:T(8,128)(2,1)}, bf16[384,512]{1,0:T(8,128)(2,1)}, bf16[384,512]{1,0:T(8,128)(2,1)}, f32[256,512]{1,0:T(8,128)S(1)}, bf16[128...) custom-call(s32[2]{0:T(128)S(1)} %pad_add_fusion.place_ref, ...), custom_call_target="tpu_custom_call" | custom-call | flops 3932160000 | bytes 13647880 | tf_op jit(solution)/shard_map/pallas_call | solution.py:383
  58.1 2.6 %collective-permute-done.14 = bf16[2,2,304,512]{3,2,1,0:T(8,128)(2,1)S(1)} collective-permute-done((bf16[2,2,304,512]{3,2,1,0:T(8,128)(2,1)}, bf16[2,2,304,512]{3,2,1,0:T(8,128)(2,1)S(1)}, u32[]{:S(2)}, u32[]{:S(2)}) %collective-permute-start.14) | collective-permute-done | bytes 1245216 | tf_op jit(solution)/shard_map/ppermute | solution.py:43
  60.8 1.7 %fusion.1 = (bf16[2,304,512]{2,1,0:T(8,128)(2,1)S(1)}, bf16[2,304,512]{2,1,0:T(8,128)(2,1)S(1)}) fusion(bf16[2,2,304,512]{3,2,1,0:T(8,128)(2,1)S(1)} %collective-permute-done.14, bf16[2,2,304,512]{3,2,1,0:T(8,128)(2,1)} %get-tuple-element.56), kind=kLoop, calls=%fused_computation.5 | loop fusion | flops 3112960 | bytes 3735552 | tf_op jit(solution)/shard_map/convert_element_type | solution.py:82
  62.5 2.7 %collective-permute-start.15 = (bf16[2,304,512]{2,1,0:T(8,128)(2,1)S(1)}, bf16[2,304,512]{2,1,0:T(8,128)(2,1)S(1)}, u32[]{:S(2)}, u32[]{:S(2)}) collective-permute-start(bf16[2,304,512]{2,1,0:T(8,128)(2,1)S(1)} %get-tuple-element.85), channel_id=1, source_target_pairs={{0,192},{1,193},{2,194},{3,195},{4,196},{5,197},{6,198},{7,199},{8... | collective-permute-start | bytes 1867784 | tf_op jit(solution)/shard_map/ppermute | solution.py:43
  65.3 0.7 collective-permute-start.18
  66.0 0.7 collective-permute-done.17.a_ref
  66.7 4.0 %collective-permute-start.19 = (bf16[128,512]{1,0:T(8,128)(2,1)S(1)}, bf16[128,512]{1,0:T(8,128)(2,1)S(1)}, u32[]{:S(2)}, u32[]{:S(2)}) collective-permute-start(bf16[128,512]{1,0:T(8,128)(2,1)S(1)} %get-tuple-element.61), channel_id=1, source_target_pairs={{0,30},{1,31},{2,4},{3,5},{4,2},{5,3},{6,8},{7,9},{8,6},{9,7},{10,... | collective-permute-start | bytes 393224 | tf_op jit(solution)/shard_map/ppermute | solution.py:43
  70.7 3.1 %collective-permute-done.19.d_ref = bf16[128,512]{1,0:T(8,128)(2,1)S(1)} collective-permute-done((bf16[128,512]{1,0:T(8,128)(2,1)S(1)}, bf16[128,512]{1,0:T(8,128)(2,1)S(1)}, u32[]{:S(2)}, u32[]{:S(2)}) %collective-permute-start.19) | collective-permute-done | bytes 131104 | tf_op jit(solution)/shard_map/ppermute | solution.py:43
  73.7 6.1 %collective-permute-done.15 = bf16[2,304,512]{2,1,0:T(8,128)(2,1)S(1)} collective-permute-done((bf16[2,304,512]{2,1,0:T(8,128)(2,1)S(1)}, bf16[2,304,512]{2,1,0:T(8,128)(2,1)S(1)}, u32[]{:S(2)}, u32[]{:S(2)}) %collective-permute-start.15) | collective-permute-done | bytes 622624 | tf_op jit(solution)/shard_map/ppermute | solution.py:43
  79.9 1.1 collective-permute-done.16
  80.9 1.1 fusion.7
  82.0 1.8 %collective-permute-start.21 = (bf16[304,512]{1,0:T(8,128)(2,1)}, bf16[304,512]{1,0:T(8,128)(2,1)}, u32[]{:S(2)}, u32[]{:S(2)}) collective-permute-start(bf16[304,512]{1,0:T(8,128)(2,1)} %get-tuple-element.68), channel_id=1, source_target_pairs={{0,64},{1,65},{2,66},{3,67},{4,68},{5,69},{6,70},{7,71},{8,72},{9,... | collective-permute-start | bytes 933896 | tf_op jit(solution)/shard_map/ppermute | solution.py:43
  83.9 0.8 collective-permute-start.22
  84.7 7.6 %collective-permute-done.21 = bf16[304,512]{1,0:T(8,128)(2,1)} collective-permute-done((bf16[304,512]{1,0:T(8,128)(2,1)}, bf16[304,512]{1,0:T(8,128)(2,1)}, u32[]{:S(2)}, u32[]{:S(2)}) %collective-permute-start.21) | collective-permute-done | bytes 311328 | tf_op jit(solution)/shard_map/ppermute | solution.py:43
  92.3 2.0 %collective-permute-done.22 = bf16[304,512]{1,0:T(8,128)(2,1)} collective-permute-done((bf16[304,512]{1,0:T(8,128)(2,1)}, bf16[304,512]{1,0:T(8,128)(2,1)}, u32[]{:S(2)}, u32[]{:S(2)}) %collective-permute-start.22) | collective-permute-done | bytes 311328 | tf_op jit(solution)/shard_map/ppermute | solution.py:43
  94.3 1.6 %fusion.13 = (bf16[304,512]{1,0:T(8,128)(2,1)S(1)}, bf16[304,512]{1,0:T(8,128)(2,1)S(1)}) fusion(bf16[304,512]{1,0:T(8,128)(2,1)} %collective-permute-done.21, bf16[2,2,304,512]{3,2,1,0:T(8,128)(2,1)S(1)} %collective-permute-done.20, bf16[2,304,512]{2,1,0:T(8,128)(2,1)} %copy-done.14, bf16[2,2,304,512]{3,2,1,0:T(8,128)(2,1)S(1)} %copy-done.11, ...), kind=kLoop, calls=%fused_computation.21 | loop fusion | flops 3424256 | bytes 3112960 | tf_op jit(solution)/shard_map/convert_element_type | solution.py:82
  96.0 0.7 copy-done.12
  97.5 0.8 slice.93
  98.3 0.8 slice.94
  99.2 4.9 %collective-permute-done.23 = bf16[8,2,16,512]{3,2,1,0:T(8,128)(2,1)S(1)} collective-permute-done((bf16[8,2,16,512]{3,2,1,0:T(8,128)(2,1)S(1)}, bf16[8,2,16,512]{3,2,1,0:T(8,128)(2,1)S(1)}, u32[]{:S(2)}, u32[]{:S(2)}) %collective-permute-start.23) | collective-permute-done | bytes 262176 | tf_op jit(solution)/shard_map/ppermute | solution.py:43
  104.3 2.5 %collective-permute-start.24 = (bf16[8,24,512]{2,1,0:T(8,128)(2,1)S(1)}, bf16[8,24,512]{2,1,0:T(8,128)(2,1)S(1)}, u32[]{:S(2)}, u32[]{:S(2)}) collective-permute-start(bf16[8,24,512]{2,1,0:T(8,128)(2,1)S(1)} %dynamic-slice_bitcast_fusion), channel_id=1, source_target_pairs={{0,2},{1,3},{2,0},{3,1},{4,6},{5,7},{6,4},{7,5},{8,10},{9,11},{10,... | collective-permute-start | bytes 589832 | tf_op jit(solution)/shard_map/ppermute | solution.py:43
  106.9 3.6 %collective-permute-done.24 = bf16[8,24,512]{2,1,0:T(8,128)(2,1)S(1)} collective-permute-done((bf16[8,24,512]{2,1,0:T(8,128)(2,1)S(1)}, bf16[8,24,512]{2,1,0:T(8,128)(2,1)S(1)}, u32[]{:S(2)}, u32[]{:S(2)}) %collective-permute-start.24) | collective-permute-done | bytes 196640 | tf_op jit(solution)/shard_map/ppermute | solution.py:43
  110.7 5.1 %collective-permute-done.25 = bf16[2,2,24,512]{3,2,1,0:T(8,128)(2,1)S(1)} collective-permute-done((bf16[2,2,24,512]{3,2,1,0:T(8,128)(2,1)S(1)}, bf16[2,2,24,512]{3,2,1,0:T(8,128)(2,1)S(1)}, u32[]{:S(2)}, u32[]{:S(2)}) %collective-permute-start.25) | collective-permute-done | bytes 98336 | tf_op jit(solution)/shard_map/ppermute | solution.py:43
  116.4 2.0 %collective-permute-start.27 = (bf16[128,512]{1,0:T(8,128)(2,1)S(1)}, bf16[128,512]{1,0:T(8,128)(2,1)S(1)}, u32[]{:S(2)}, u32[]{:S(2)}) collective-permute-start(bf16[128,512]{1,0:T(8,128)(2,1)S(1)} %get-tuple-element.72), channel_id=1, source_target_pairs={{0,2},{1,3},{2,0},{3,1},{4,6},{5,7},{6,4},{7,5},{8,10},{9,11},{10,... | collective-permute-start | bytes 393224 | tf_op jit(solution)/shard_map/ppermute | solution.py:43
  118.5 2.5 %collective-permute-done.26 = bf16[2,24,512]{2,1,0:T(8,128)(2,1)S(1)} collective-permute-done((bf16[2,24,512]{2,1,0:T(8,128)(2,1)S(1)}, bf16[2,24,512]{2,1,0:T(8,128)(2,1)S(1)}, u32[]{:S(2)}, u32[]{:S(2)}) %collective-permute-start.26) | collective-permute-done | bytes 49184 | tf_op jit(solution)/shard_map/ppermute | solution.py:43
  121.4 4.7 %collective-permute-start.28 = (bf16[24,512]{1,0:T(8,128)(2,1)S(1)}, bf16[24,512]{1,0:T(8,128)(2,1)S(1)}, u32[]{:S(2)}, u32[]{:S(2)}) collective-permute-start(bf16[24,512]{1,0:T(8,128)(2,1)S(1)} %get-tuple-element.86), channel_id=1, source_target_pairs={{0,16},{1,17},{2,18},{3,19},{4,20},{5,21},{6,22},{7,23},{8,24},{9,... | collective-permute-start | bytes 73736 | tf_op jit(solution)/shard_map/ppermute | solution.py:43
  126.1 3.0 %collective-permute-done.28.got_ref = bf16[24,512]{1,0:T(8,128)(2,1)S(1)} collective-permute-done((bf16[24,512]{1,0:T(8,128)(2,1)S(1)}, bf16[24,512]{1,0:T(8,128)(2,1)S(1)}, u32[]{:S(2)}, u32[]{:S(2)}) %collective-permute-start.28) | collective-permute-done | bytes 24608 | tf_op jit(solution)/shard_map/ppermute | solution.py:43
  129.2 1.5 %shard_map.192 = (bf16[256,512]{1,0:T(8,128)(2,1)}, f32[14,512]{1,0:T(8,128)S(1)}, f32[2,512]{1,0:T(2,128)}) custom-call(s32[1,128]{1,0:T(1,128)S(1)} %bitcast.75, s32[1,8]{1,0:T(1,128)S(1)} %bitcast.77, f32[256,512]{1,0:T(8,128)S(1)} %get-tuple-element.55.own_ref, bf16[128,512]{1,0:T(8,128)(2,1)S(1)} %collective-permute-done.17.a_ref, ...), custom_call_target="tpu_custom_call" | custom-call | flops 134217728 | bytes 1393184 | tf_op jit(solution)/shard_map/pallas_call | solution.py:383
  (87 shorter events, 6.0 us)
Async XLA Ops:
  0.6 40.9 %copy-start.16 = (s32[1,1,384]{2,1,0:T(1,128)S(1)}, s32[1,1,384]{2,1,0:T(1,128)}, u32[]{:S(2)}) copy-start(s32[1,1,384]{2,1,0:T(1,128)} %param.17) | copy-start | bytes 4612
  0.6 40.9 %copy-start.17 = (s32[1,1,384]{2,1,0:T(1,128)S(1)}, s32[1,1,384]{2,1,0:T(1,128)}, u32[]{:S(2)}) copy-start(s32[1,1,384]{2,1,0:T(1,128)} %param.18) | copy-start | bytes 4612
  0.7 42.4 %copy-start.9 = (f32[512]{0:T(512)S(1)}, f32[512]{0:T(512)}, u32[]{:S(2)}) copy-start(f32[512]{0:T(512)} %param.26) | copy-start | bytes 6148
  0.7 1.0 copy-start
  1.6 0.7 copy-start.2
  2.3 0.7 copy-start.4
  2.9 38.6 %copy-start.18 = (s32[1,1,384]{2,1,0:T(1,128)S(1)}, s32[1,1,384]{2,1,0:T(1,128)}, u32[]{:S(2)}) copy-start(s32[1,1,384]{2,1,0:T(1,128)} %param.19) | copy-start | bytes 4612
  2.9 40.1 %copy-start.1 = (bf16[1,1,1,256,512]{4,3,2,1,0:T(8,128)(2,1)S(1)}, bf16[1,1,1,256,512]{4,3,2,1,0:T(8,128)(2,1)}, u32[]{:S(2)}) copy-start(bf16[1,1,1,256,512]{4,3,2,1,0:T(8,128)(2,1)} %param.15) | copy-start | bytes 786436
  3.0 40.1 %copy-start.6 = (bf16[1,1,1,384,512]{4,3,2,1,0:T(8,128)(2,1)S(1)}, bf16[1,1,1,384,512]{4,3,2,1,0:T(8,128)(2,1)}, u32[]{:S(2)}) copy-start(bf16[1,1,1,384,512]{4,3,2,1,0:T(8,128)(2,1)} %param.16) | copy-start | bytes 1179652
  3.0 40.1 %copy-start.7 = (bf16[1,1,1,384,512]{4,3,2,1,0:T(8,128)(2,1)S(1)}, bf16[1,1,1,384,512]{4,3,2,1,0:T(8,128)(2,1)}, u32[]{:S(2)}) copy-start(bf16[1,1,1,384,512]{4,3,2,1,0:T(8,128)(2,1)} %param.29) | copy-start | bytes 1179652
  3.0 40.1 %copy-start.8 = (bf16[1,1,1,256,512]{4,3,2,1,0:T(8,128)(2,1)S(1)}, bf16[1,1,1,256,512]{4,3,2,1,0:T(8,128)(2,1)}, u32[]{:S(2)}) copy-start(bf16[1,1,1,256,512]{4,3,2,1,0:T(8,128)(2,1)} %param.28) | copy-start | bytes 786436
  3.4 9.4 %collective-permute-start = (bf16[8,512]{1,0:T(8,128)(2,1)S(1)}, bf16[8,512]{1,0:T(8,128)(2,1)S(1)}, u32[]{:S(2)}, u32[]{:S(2)}) collective-permute-start(bf16[8,512]{1,0:T(8,128)(2,1)S(1)} %get-tuple-element.43), channel_id=1, source_target_pairs={{0,2},{1,3},{2,0},{3,1},{4,6},{5,7},{6,4},{7,5},{8,10},{9,11},{10,... | collective-permute-start | bytes 24584 | tf_op jit(solution)/shard_map/ppermute | solution.py:43
  4.7 11.8 %collective-permute-start.2 = (bf16[128,512]{1,0:T(8,128)(2,1)S(1)}, bf16[128,512]{1,0:T(8,128)(2,1)S(1)}, u32[]{:S(2)}, u32[]{:S(2)}) collective-permute-start(bf16[128,512]{1,0:T(8,128)(2,1)S(1)} %get-tuple-element.47), channel_id=1, source_target_pairs={{0,2},{1,3},{2,0},{3,1},{4,6},{5,7},{6,4},{7,5},{8,10},{9,11},{10,... | collective-permute-start | bytes 393224 | tf_op jit(solution)/shard_map/ppermute | solution.py:43
  5.5 11.1 %collective-permute-start.3 = (bf16[128,512]{1,0:T(8,128)(2,1)S(1)}, bf16[128,512]{1,0:T(8,128)(2,1)S(1)}, u32[]{:S(2)}, u32[]{:S(2)}) collective-permute-start(bf16[128,512]{1,0:T(8,128)(2,1)S(1)} %get-tuple-element.47), channel_id=1, source_target_pairs={{32,64},{33,65},{34,66},{35,67},{36,68},{37,69},{38,70},{39,71},{4... | collective-permute-start | bytes 393224 | tf_op jit(solution)/shard_map/ppermute | solution.py:43
  6.1 10.4 %collective-permute-start.4 = (bf16[128,512]{1,0:T(8,128)(2,1)S(1)}, bf16[128,512]{1,0:T(8,128)(2,1)S(1)}, u32[]{:S(2)}, u32[]{:S(2)}) collective-permute-start(bf16[128,512]{1,0:T(8,128)(2,1)S(1)} %get-tuple-element.47), channel_id=1, source_target_pairs={{0,30},{1,31},{2,4},{3,5},{4,2},{5,3},{6,8},{7,9},{8,6},{9,7},{10,... | collective-permute-start | bytes 393224 | tf_op jit(solution)/shard_map/ppermute | solution.py:43
  12.8 3.7 %collective-permute-start.1 = (bf16[16,512]{1,0:T(8,128)(2,1)S(1)}, bf16[16,512]{1,0:T(8,128)(2,1)S(1)}, u32[]{:S(2)}, u32[]{:S(2)}) collective-permute-start(bf16[16,512]{1,0:T(8,128)(2,1)S(1)} %pad_maximum_fusion.6), channel_id=1, source_target_pairs={{0,4},{1,5},{2,6},{3,7},{4,0},{5,1},{6,2},{7,3},{8,12},{9,13},{10,... | collective-permute-start | bytes 49160 | tf_op jit(solution)/shard_map/ppermute | solution.py:43
  16.6 5.2 %collective-permute-start.5 = (bf16[32,512]{1,0:T(8,128)(2,1)S(1)}, bf16[32,512]{1,0:T(8,128)(2,1)S(1)}, u32[]{:S(2)}, u32[]{:S(2)}) collective-permute-start(bf16[32,512]{1,0:T(8,128)(2,1)S(1)} %pad_maximum_fusion.5), channel_id=1, source_target_pairs={{0,28},{1,29},{2,30},{3,31},{4,8},{5,9},{6,10},{7,11},{8,4},{9,5},... | collective-permute-start | bytes 98312 | tf_op jit(solution)/shard_map/ppermute | solution.py:43
  21.8 6.9 %collective-permute-start.7 = (bf16[64,512]{1,0:T(8,128)(2,1)S(1)}, bf16[64,512]{1,0:T(8,128)(2,1)S(1)}, u32[]{:S(2)}, u32[]{:S(2)}) collective-permute-start(bf16[64,512]{1,0:T(8,128)(2,1)S(1)} %constant_dynamic-update-slice_fusion), channel_id=1, source_target_pairs={{0,12},{1,13},{2,14},{3,15},{4,24},{5,25},{6,26},{7,27},{8,20},{9,... | collective-permute-start | bytes 196616 | tf_op jit(solution)/shard_map/ppermute | solution.py:43
  22.9 9.0 %collective-permute-start.6 = (bf16[64,512]{1,0:T(8,128)(2,1)S(1)}, bf16[64,512]{1,0:T(8,128)(2,1)S(1)}, u32[]{:S(2)}, u32[]{:S(2)}) collective-permute-start(bf16[64,512]{1,0:T(8,128)(2,1)S(1)} %constant_dynamic-update-slice_fusion), channel_id=1, source_target_pairs={{0,64},{1,65},{2,66},{3,67},{4,68},{5,69},{6,70},{7,71},{8,72},{9,... | collective-permute-start | bytes 196616 | tf_op jit(solution)/shard_map/ppermute | solution.py:43
  28.7 5.5 %collective-permute-start.8 = (bf16[64,512]{1,0:T(8,128)(2,1)S(1)}, bf16[64,512]{1,0:T(8,128)(2,1)S(1)}, u32[]{:S(2)}, u32[]{:S(2)}) collective-permute-start(bf16[64,512]{1,0:T(8,128)(2,1)S(1)} %collective-permute-done.7), channel_id=1, source_target_pairs={{0,192},{1,193},{2,194},{3,195},{4,196},{5,197},{6,198},{7,199},{8... | collective-permute-start | bytes 196616 | tf_op jit(solution)/shard_map/ppermute | solution.py:43
  34.2 5.1 %collective-permute-start.11 = (bf16[128,512]{1,0:T(8,128)(2,1)S(1)}, bf16[128,512]{1,0:T(8,128)(2,1)S(1)}, u32[]{:S(2)}, u32[]{:S(2)}) collective-permute-start(bf16[128,512]{1,0:T(8,128)(2,1)S(1)} %pad_maximum_fusion.3), channel_id=1, source_target_pairs={{0,64},{1,65},{2,66},{3,67},{4,68},{5,69},{6,70},{7,71},{8,72},{9,... | collective-permute-start | bytes 393224 | tf_op jit(solution)/shard_map/ppermute | solution.py:43
  35.0 6.3 %collective-permute-start.10 = (bf16[128,512]{1,0:T(8,128)(2,1)S(1)}, bf16[128,512]{1,0:T(8,128)(2,1)S(1)}, u32[]{:S(2)}, u32[]{:S(2)}) collective-permute-start(bf16[128,512]{1,0:T(8,128)(2,1)S(1)} %pad_maximum_fusion.2), channel_id=1, source_target_pairs={{0,192},{1,193},{2,194},{3,195},{4,196},{5,197},{6,198},{7,199},{8... | collective-permute-start | bytes 393224 | tf_op jit(solution)/shard_map/ppermute | solution.py:43
  37.6 4.8 %collective-permute-start.9 = (bf16[128,512]{1,0:T(8,128)(2,1)S(1)}, bf16[128,512]{1,0:T(8,128)(2,1)S(1)}, u32[]{:S(2)}, u32[]{:S(2)}) collective-permute-start(bf16[128,512]{1,0:T(8,128)(2,1)S(1)} %get-tuple-element.47), channel_id=1, source_target_pairs={{0,32},{1,33},{2,34},{3,35},{4,36},{5,37},{6,38},{7,39},{8,40},{9,... | collective-permute-start | bytes 393224 | tf_op jit(solution)/shard_map/ppermute | solution.py:43
  39.3 3.2 %collective-permute-start.13 = (bf16[256,512]{1,0:T(8,128)(2,1)S(1)}, bf16[256,512]{1,0:T(8,128)(2,1)S(1)}, u32[]{:S(2)}, u32[]{:S(2)}) collective-permute-start(bf16[256,512]{1,0:T(8,128)(2,1)S(1)} %constant_dynamic-update-slice_fusion.4.near_low_hbm), channel_id=1, source_target_pairs={{0,32},{1,33},{2,34},{3,35},{4,36},{5,37},{6,38},{7,39},{8,40},{9,... | collective-permute-start | bytes 786440 | tf_op jit(solution)/shard_map/ppermute | solution.py:43
  41.3 1.8 %collective-permute-start.12 = (bf16[256,512]{1,0:T(8,128)(2,1)S(1)}, bf16[256,512]{1,0:T(8,128)(2,1)S(1)}, u32[]{:S(2)}, u32[]{:S(2)}) collective-permute-start(bf16[256,512]{1,0:T(8,128)(2,1)S(1)} %constant_dynamic-update-slice_fusion.2.near_top_hbm), channel_id=1, source_target_pairs={{0,32},{1,33},{2,34},{3,35},{4,36},{5,37},{6,38},{7,39},{8,40},{9,... | collective-permute-start | bytes 786440 | tf_op jit(solution)/shard_map/ppermute | solution.py:43
  43.1 0.7 copy-start.10
  57.5 3.2 %collective-permute-start.14 = (bf16[2,2,304,512]{3,2,1,0:T(8,128)(2,1)}, bf16[2,2,304,512]{3,2,1,0:T(8,128)(2,1)S(1)}, u32[]{:S(2)}, u32[]{:S(2)}) collective-permute-start(bf16[2,2,304,512]{3,2,1,0:T(8,128)(2,1)} %get-tuple-element.57), channel_id=1, source_target_pairs={{0,32},{1,33},{2,34},{3,35},{4,36},{5,37},{6,38},{7,39},{8,40},{9,... | collective-permute-start | bytes 3735560 | tf_op jit(solution)/shard_map/ppermute | solution.py:43
  57.7 23.2 %collective-permute-start.20 = (bf16[2,2,304,512]{3,2,1,0:T(8,128)(2,1)}, bf16[2,2,304,512]{3,2,1,0:T(8,128)(2,1)S(1)}, u32[]{:S(2)}, u32[]{:S(2)}) collective-permute-start(bf16[2,2,304,512]{3,2,1,0:T(8,128)(2,1)} %get-tuple-element.65), channel_id=1, source_target_pairs={{0,32},{1,33},{2,34},{3,35},{4,36},{5,37},{6,38},{7,39},{8,40},{9,... | collective-permute-start | bytes 3735560 | tf_op jit(solution)/shard_map/ppermute | solution.py:43
  60.8 20.2 %copy-start.11 = (bf16[2,2,304,512]{3,2,1,0:T(8,128)(2,1)S(1)}, bf16[2,2,304,512]{3,2,1,0:T(8,128)(2,1)}, u32[]{:S(2)}) copy-start(bf16[2,2,304,512]{3,2,1,0:T(8,128)(2,1)} %get-tuple-element.64) | copy-start | bytes 3735556
  62.5 17.4 %collective-permute-start.15 = (bf16[2,304,512]{2,1,0:T(8,128)(2,1)S(1)}, bf16[2,304,512]{2,1,0:T(8,128)(2,1)S(1)}, u32[]{:S(2)}, u32[]{:S(2)}) collective-permute-start(bf16[2,304,512]{2,1,0:T(8,128)(2,1)S(1)} %get-tuple-element.85), channel_id=1, source_target_pairs={{0,192},{1,193},{2,194},{3,195},{4,196},{5,197},{6,198},{7,199},{8... | collective-permute-start | bytes 1867784 | tf_op jit(solution)/shard_map/ppermute | solution.py:43
  65.1 15.8 %collective-permute-start.16 = (bf16[2,304,512]{2,1,0:T(8,128)(2,1)S(1)}, bf16[2,304,512]{2,1,0:T(8,128)(2,1)S(1)}, u32[]{:S(2)}, u32[]{:S(2)}) collective-permute-start(bf16[2,304,512]{2,1,0:T(8,128)(2,1)S(1)} %get-tuple-element.84), channel_id=1, source_target_pairs={{0,64},{1,65},{2,66},{3,67},{4,68},{5,69},{6,70},{7,71},{8,72},{9,... | collective-permute-start | bytes 1867784 | tf_op jit(solution)/shard_map/ppermute | solution.py:43
  65.3 1.3 %collective-permute-start.17 = (bf16[128,512]{1,0:T(8,128)(2,1)S(1)}, bf16[128,512]{1,0:T(8,128)(2,1)S(1)}, u32[]{:S(2)}, u32[]{:S(2)}) collective-permute-start(bf16[128,512]{1,0:T(8,128)(2,1)S(1)} %get-tuple-element.59), channel_id=1, source_target_pairs={{0,32},{1,33},{2,34},{3,35},{4,36},{5,37},{6,38},{7,39},{8,40},{9,... | collective-permute-start | bytes 393224 | tf_op jit(solution)/shard_map/ppermute | solution.py:43
  65.3 5.3 %collective-permute-start.18 = (bf16[128,512]{1,0:T(8,128)(2,1)S(1)}, bf16[128,512]{1,0:T(8,128)(2,1)S(1)}, u32[]{:S(2)}, u32[]{:S(2)}) collective-permute-start(bf16[128,512]{1,0:T(8,128)(2,1)S(1)} %get-tuple-element.60), channel_id=1, source_target_pairs={{32,64},{33,65},{34,66},{35,67},{36,68},{37,69},{38,70},{39,71},{4... | collective-permute-start | bytes 393224 | tf_op jit(solution)/shard_map/ppermute | solution.py:43
  66.7 7.1 %collective-permute-start.19 = (bf16[128,512]{1,0:T(8,128)(2,1)S(1)}, bf16[128,512]{1,0:T(8,128)(2,1)S(1)}, u32[]{:S(2)}, u32[]{:S(2)}) collective-permute-start(bf16[128,512]{1,0:T(8,128)(2,1)S(1)} %get-tuple-element.61), channel_id=1, source_target_pairs={{0,30},{1,31},{2,4},{3,5},{4,2},{5,3},{6,8},{7,9},{8,6},{9,7},{10,... | collective-permute-start | bytes 393224 | tf_op jit(solution)/shard_map/ppermute | solution.py:43
  79.9 2.2 %copy-start.14 = (bf16[2,304,512]{2,1,0:T(8,128)(2,1)}, bf16[2,304,512]{2,1,0:T(8,128)(2,1)S(1)}, u32[]{:S(2)}) copy-start(bf16[2,304,512]{2,1,0:T(8,128)(2,1)S(1)} %collective-permute-done.15) | copy-start | bytes 1867780
  80.9 1.1 copy-start.15
  82.0 10.2 %collective-permute-start.21 = (bf16[304,512]{1,0:T(8,128)(2,1)}, bf16[304,512]{1,0:T(8,128)(2,1)}, u32[]{:S(2)}, u32[]{:S(2)}) collective-permute-start(bf16[304,512]{1,0:T(8,128)(2,1)} %get-tuple-element.68), channel_id=1, source_target_pairs={{0,64},{1,65},{2,66},{3,67},{4,68},{5,69},{6,70},{7,71},{8,72},{9,... | collective-permute-start | bytes 933896 | tf_op jit(solution)/shard_map/ppermute | solution.py:43
  83.9 10.4 %collective-permute-start.22 = (bf16[304,512]{1,0:T(8,128)(2,1)}, bf16[304,512]{1,0:T(8,128)(2,1)}, u32[]{:S(2)}, u32[]{:S(2)}) collective-permute-start(bf16[304,512]{1,0:T(8,128)(2,1)} %get-tuple-element.69), channel_id=1, source_target_pairs={{0,192},{1,193},{2,194},{3,195},{4,196},{5,197},{6,198},{7,199},{8... | collective-permute-start | bytes 933896 | tf_op jit(solution)/shard_map/ppermute | solution.py:43
  95.9 0.7 copy-start.12
  95.9 0.8 copy-start.13
  97.1 7.0 %collective-permute-start.23 = (bf16[8,2,16,512]{3,2,1,0:T(8,128)(2,1)S(1)}, bf16[8,2,16,512]{3,2,1,0:T(8,128)(2,1)S(1)}, u32[]{:S(2)}, u32[]{:S(2)}) collective-permute-start(bf16[8,2,16,512]{3,2,1,0:T(8,128)(2,1)S(1)} %fusion.19), channel_id=1, source_target_pairs={{0,3},{1,2},{2,1},{3,0},{4,7},{5,6},{6,5},{7,4},{8,11},{9,10},{10,... | collective-permute-start | bytes 786440 | tf_op jit(solution)/shard_map/ppermute | solution.py:43
  104.3 24.9 %copy-start.3 = (s32[1,1,128]{2,1,0:T(1,128)S(1)}, s32[1,1,128]{2,1,0:T(1,128)}, u32[]{:S(2)}) copy-start(s32[1,1,128]{2,1,0:T(1,128)} %param.20) | copy-start | bytes 1540
  104.3 24.9 %copy-start.5 = (s32[1,1,8]{2,1,0:T(1,128)S(1)}, s32[1,1,8]{2,1,0:T(1,128)}, u32[]{:S(2)}) copy-start(s32[1,1,8]{2,1,0:T(1,128)} %param.21) | copy-start | bytes 100
  104.3 6.2 %collective-permute-start.24 = (bf16[8,24,512]{2,1,0:T(8,128)(2,1)S(1)}, bf16[8,24,512]{2,1,0:T(8,128)(2,1)S(1)}, u32[]{:S(2)}, u32[]{:S(2)}) collective-permute-start(bf16[8,24,512]{2,1,0:T(8,128)(2,1)S(1)} %dynamic-slice_bitcast_fusion), channel_id=1, source_target_pairs={{0,2},{1,3},{2,0},{3,1},{4,6},{5,7},{6,4},{7,5},{8,10},{9,11},{10,... | collective-permute-start | bytes 589832 | tf_op jit(solution)/shard_map/ppermute | solution.py:43
  110.6 5.2 %collective-permute-start.25 = (bf16[2,2,24,512]{3,2,1,0:T(8,128)(2,1)S(1)}, bf16[2,2,24,512]{3,2,1,0:T(8,128)(2,1)S(1)}, u32[]{:S(2)}, u32[]{:S(2)}) collective-permute-start(bf16[2,2,24,512]{3,2,1,0:T(8,128)(2,1)S(1)} %dynamic-slice_bitcast_fusion.1), channel_id=1, source_target_pairs={{0,4},{1,5},{2,6},{3,7},{4,0},{5,1},{6,2},{7,3},{8,12},{9,13},{10,... | collective-permute-start | bytes 294920 | tf_op jit(solution)/shard_map/ppermute | solution.py:43
  115.9 5.1 %collective-permute-start.26 = (bf16[2,24,512]{2,1,0:T(8,128)(2,1)S(1)}, bf16[2,24,512]{2,1,0:T(8,128)(2,1)S(1)}, u32[]{:S(2)}, u32[]{:S(2)}) collective-permute-start(bf16[2,24,512]{2,1,0:T(8,128)(2,1)S(1)} %dynamic-slice_bitcast_fusion.2), channel_id=1, source_target_pairs={{0,8},{1,9},{2,10},{3,11},{4,12},{5,13},{6,14},{7,15},{8,0},{9,1},... | collective-permute-start | bytes 147464 | tf_op jit(solution)/shard_map/ppermute | solution.py:43
  116.4 5.0 %collective-permute-start.27 = (bf16[128,512]{1,0:T(8,128)(2,1)S(1)}, bf16[128,512]{1,0:T(8,128)(2,1)S(1)}, u32[]{:S(2)}, u32[]{:S(2)}) collective-permute-start(bf16[128,512]{1,0:T(8,128)(2,1)S(1)} %get-tuple-element.72), channel_id=1, source_target_pairs={{0,2},{1,3},{2,0},{3,1},{4,6},{5,7},{6,4},{7,5},{8,10},{9,11},{10,... | collective-permute-start | bytes 393224 | tf_op jit(solution)/shard_map/ppermute | solution.py:43
  121.4 7.7 %collective-permute-start.28 = (bf16[24,512]{1,0:T(8,128)(2,1)S(1)}, bf16[24,512]{1,0:T(8,128)(2,1)S(1)}, u32[]{:S(2)}, u32[]{:S(2)}) collective-permute-start(bf16[24,512]{1,0:T(8,128)(2,1)S(1)} %get-tuple-element.86), channel_id=1, source_target_pairs={{0,16},{1,17},{2,18},{3,19},{4,20},{5,21},{6,22},{7,23},{8,24},{9,... | collective-permute-start | bytes 73736 | tf_op jit(solution)/shard_map/ppermute | solution.py:43
